TPU v7x, 512 devices: a whole 4x4x16 slice. The times are simulated.
512 devices in a mesh: node: 128 (over z, x, y_lo), rep: 4 (over y_hi, core).
Axes of the slice: x: 4, y: 4 (y_hi: 2, y_lo: 2; y = y_hi * 2 + y_lo), z: 16, core: 2. Of those that a mesh axis runs over, the one named last changes fastest.
Arguments:
- features: bfloat16 [16384, 256], P('node'), may hold values from -6 to 6
- weight: bfloat16 [256, 256], replicated, may hold values from -0.375 to 0.375
- out_grad: bfloat16 [16384, 256], P('node'), may hold values from -6 to 6
- tile_place: int32 [128, 4, 32], P('node', 'rep'), may hold values from 0 to 32, as said below
- tile_bits: int32 [128, 4, 32, 16, 128], P('node', 'rep'), may hold values from 0 to 255, as said below
- back_place: int32 [128, 4, 32], P('node', 'rep'), may hold values from 0 to 32, as said below
- back_bits: int32 [128, 4, 32, 16, 128], P('node', 'rep'), may hold values from 0 to 255, as said below
Outputs:
- activation: bfloat16 [16384, 256], P('node')
- weight_grad: float32 [256, 256], replicated
- input_grad: bfloat16 [16384, 256], P('node')
Inputs may be any that keep to these rules, and one draw needn't show every extreme that they name: `tile_place`: in each shard the positions of its nonzero tiles stand first in ascending order, then every remaining slot holds 32; the shard of node index 0 and rep index 0 has all 32 tiles nonzero. `tile_bits`: slots holding 32 in tile_place have all words 0. `back_place`: as tile_place, for the transposed adjacency; the shard of node index 0 and rep index 0 is full. `back_bits`: slots holding 32 in back_place have all words 0; the tiles are the transposes of those of tile_bits.
All inputs are finite; a program needn't handle non-finite values.
Results may differ from a plain program's by a relative error of at most 0.0058.
Values may be sent and summed in bfloat16 or wider, within the bound.
No kernel may reach another device: no remote copies, remote signals or barrier semaphores. Data moves between devices by JAX's collectives and lax.ppermute only.
A program may use at most 64 MiB of HBM per device.

v0:
```python
import jax
import jax.numpy as jnp
from jax import lax
from jax.sharding import PartitionSpec as P


def passed_along(array, axis, by):
    size = lax.axis_size(axis)
    pairs = [(i, i + by) for i in range(size) if 0 <= i + by < size]
    return lax.ppermute(array, axis, pairs)


def dense_block(positions, packed, row_count, section_total):
    tile_count = row_count // 128
    per_section = tile_count * tile_count
    shifts = jnp.arange(8, dtype=jnp.int32)
    pattern = jnp.bitwise_and(jnp.right_shift(packed[:, :, None, :], shifts[:, None]), 1)
    pattern = pattern.reshape(packed.shape[0], 128, 128).astype(jnp.bfloat16)
    local = positions % per_section
    row_line = jnp.arange(tile_count, dtype=jnp.int32)
    col_line = jnp.arange(section_total * tile_count, dtype=jnp.int32)
    col_index = positions // per_section * tile_count + local % tile_count
    rows_hot = ((local // tile_count)[:, None] == row_line[None, :]).astype(jnp.bfloat16)
    cols_hot = (col_index[:, None] == col_line[None, :]).astype(jnp.bfloat16)
    dense = jnp.einsum(
        "pa,pc,pvu->aucv", rows_hot, cols_hot, pattern, preferred_element_type=jnp.float32
    ).astype(jnp.bfloat16)
    return dense.reshape(row_count, section_total * row_count)


def quarter_share(value, mover):
    replicas = lax.axis_size("rep")
    quarter = value.shape[0] // replicas
    own = lax.axis_index("node") % replicas
    rep_index = lax.axis_index("rep")
    result = lax.dynamic_slice_in_dim(value, own * quarter, quarter, 0)
    for offset in range(1 - replicas, replicas):
        if offset == 0:
            continue
        start = jnp.clip(own + offset, 0, replicas - 1) * quarter
        outgoing = lax.dynamic_slice_in_dim(value, start, quarter, 0)
        incoming = mover(outgoing, offset)
        result = jnp.where(own - rep_index == offset, incoming, result)
    return result


def per_device(features, weight, out_grad, tile_place, tile_bits, back_place, back_bits):
    row_count = features.shape[0]
    replicas = lax.axis_size("rep")
    section_total = lax.axis_size("node") // replicas

    def fold_with(dense, piece):
        return jnp.dot(dense, piece, preferred_element_type=jnp.float32)

    forward_dense = dense_block(
        tile_place.reshape(-1),
        tile_bits.reshape((-1,) + tile_bits.shape[-2:]),
        row_count,
        section_total,
    )
    feature_piece = quarter_share(
        features, lambda outgoing, offset: passed_along(outgoing, "node", offset)
    )
    partial_sum = fold_with(
        forward_dense, lax.all_gather(feature_piece, "node", axis=0, tiled=True)
    )
    column_ones = jnp.ones((forward_dense.shape[1],), jnp.bfloat16)
    degree_part = jnp.dot(forward_dense, column_ones, preferred_element_type=jnp.float32)
    gathered, counted = lax.psum((partial_sum, degree_part), "rep")
    scaling = lax.rsqrt(1.0 + counted)[:, None]
    hidden = (features.astype(jnp.float32) + gathered * scaling).astype(jnp.bfloat16)
    logits = jnp.dot(hidden, weight, preferred_element_type=jnp.float32)
    sigmoid_part = jax.nn.sigmoid(logits)
    activated = (logits * sigmoid_part).astype(jnp.bfloat16)
    upstream = (
        out_grad.astype(jnp.float32) * sigmoid_part * (1.0 + logits * (1.0 - sigmoid_part))
    ).astype(jnp.bfloat16)
    weight_term = lax.dot_general(
        hidden, upstream, (((0,), (0,)), ((), ())), preferred_element_type=jnp.float32
    )
    hidden_grad = lax.dot_general(
        upstream, weight, (((1,), (1,)), ((), ())), preferred_element_type=jnp.float32
    )
    pushed = (hidden_grad * scaling).astype(jnp.bfloat16)
    weight_grad = lax.psum(weight_term, "node")
    backward_dense = dense_block(
        back_place.reshape(-1),
        back_bits.reshape((-1,) + back_bits.shape[-2:]),
        row_count,
        section_total,
    )
    grad_piece = quarter_share(
        pushed, lambda outgoing, offset: passed_along(outgoing, "node", offset)
    )
    back_part = fold_with(backward_dense, lax.all_gather(grad_piece, "node", axis=0, tiled=True))
    back_total = lax.psum(back_part, "rep")
    input_grad = (hidden_grad + back_total).astype(jnp.bfloat16)
    return (activated, weight_grad, input_grad)


def solution(mesh):
    return jax.shard_map(
        per_device,
        mesh=mesh,
        in_specs=(
            P("node", None),
            P(),
            P("node", None),
            P("node", "rep", None),
            P("node", "rep", None, None, None),
            P("node", "rep", None),
            P("node", "rep", None, None, None),
        ),
        out_specs=(P("node", None), P(), P("node", None)),
        check_vma=False,
    )
```

profile of v0, /device:TPU:24, one launch (start us, length us, event | category | flops | bytes accessed | tf_op | source)
XLA Modules:
  0.0 2430.9 jit_solution(9446247461527966378)
XLA Ops:
  8.1 5.1 collective-permute-start
  13.2 2.5 collective-permute-start.1
  15.7 3.2 collective-permute-start.2
  19.0 2.6 collective-permute-start.3
  21.6 1.3 collective-permute-start.4
  22.9 1.3 collective-permute-start.5
  24.3 1.4 collective-permute-done.3
  25.6 1.6 collective-permute-done.4
  27.2 4.2 collective-permute-done.5
  31.4 1.3 select_select_fusion.1
  32.8 1.0 copy.14
  34.0 1.0 copy.12
  36.7 7.3 psum.29
  44.0 583.3 %all-gather.3.cloned.1.call-done = bf16[4096,256]{1,0:T(8,128)(2,1)} async-done(((bf16[32,256]{1,0:T(8,128)(2,1)}), bf16[4096,256]{1,0:T(8,128)(2,1)}) %all-gather.3.cloned.1.call-update) | async-done | bytes 2097168 | tf_op jit(solution)/shard_map/all_gather | solution.py:65
  627.3 2.8 fusion.22
  630.1 51.8 %all-reduce.4.cloned.1.call-done = f32[128,256]{1,0:T(8,128)} async-done(((f32[128,256]{1,0:T(8,128)}), f32[128,256]{1,0:T(8,128)}) %all-reduce.4.cloned.1.call-update) | async-done | bytes 131088 | tf_op jit(solution)/shard_map/psum | solution.py:69
  681.9 1.0 add_convert_fusion.1
  684.0 4.3 collective-permute-start.6
  688.3 2.5 collective-permute-start.7
  690.8 3.9 collective-permute-start.8
  694.7 1.9 collective-permute-start.9
  696.7 1.3 collective-permute-start.10
  698.0 1.3 collective-permute-start.11
  699.3 2.0 collective-permute-done.9
  701.3 1.0 collective-permute-done.10
  702.3 4.9 collective-permute-done.11
  708.7 590.9 %all-gather.5.cloned.1.call-done = bf16[4096,256]{1,0:T(8,128)(2,1)} async-done(((bf16[32,256]{1,0:T(8,128)(2,1)}), bf16[4096,256]{1,0:T(8,128)(2,1)}) %all-gather.5.cloned.1.call-update) | async-done | bytes 2097168 | tf_op jit(solution)/shard_map/all_gather | solution.py:95
  1299.6 2.8 fusion.24
  1303.4 50.4 %all-reduce.8.cloned.1.call-done = f32[128,256]{1,0:T(8,128)} async-done(((f32[128,256]{1,0:T(8,128)}), f32[128,256]{1,0:T(8,128)}) %all-reduce.8.cloned.1.call-update) | async-done | bytes 131088 | tf_op jit(solution)/shard_map/psum | solution.py:96
  1353.8 1.5 add_convert_fusion
  1355.3 1067.4 %all-reduce.6.cloned.1.call-done = f32[256,256]{1,0:T(8,128)} async-done(((f32[256,256]{1,0:T(8,128)}), f32[256,256]{1,0:T(8,128)}) %all-reduce.6.cloned.1.call-update) | async-done | bytes 262160 | tf_op jit(solution)/shard_map/psum | solution.py:85
  2422.7 1.7 copy.19
  (41 shorter events, 6.4 us)
Async XLA Ops:
  7.2 675.7 %copy-start = (bf16[256,256]{1,0:T(8,128)(2,1)S(1)}, bf16[256,256]{1,0:T(8,128)(2,1)}, u32[]{:S(2)}) copy-start(bf16[256,256]{1,0:T(8,128)(2,1)} %param.8) | copy-start | bytes 393220
  7.2 620.1 %all-gather.3.cloned.1.call-start = ((), (), s32[]{:S(2)}) async-start(), calls=%async_computation | async-start | bytes 2113536 | tf_op jit(solution)/shard_map/all_gather | solution.py:65
  7.2 28.4 %copy-start.2 = (s32[1,1,32]{2,1,0:T(1,128)S(1)}, s32[1,1,32]{2,1,0:T(1,128)}, u32[]{:S(2)}) copy-start(s32[1,1,32]{2,1,0:T(1,128)} %param.10) | copy-start | bytes 388
  8.1 14.8 collective-permute-start
  13.2 11.0 collective-permute-start.1
  15.7 8.5 collective-permute-start.2
  19.0 6.7 collective-permute-start.3
  21.6 5.6 collective-permute-start.4
  22.9 8.5 collective-permute-start.5
  32.8 649.1 %all-reduce.4.cloned.1.call-start = ((), (), s32[]{:S(2)}) async-start(), calls=%async_computation.1 | async-start | bytes 262144 | tf_op jit(solution)/shard_map/psum | solution.py:69
  36.5 645.4 %copy-start.1 = (bf16[128,256]{1,0:T(8,128)(2,1)S(1)}, bf16[128,256]{1,0:T(8,128)(2,1)}, u32[]{:S(2)}) copy-start(bf16[128,256]{1,0:T(8,128)(2,1)} %param.7) | copy-start | bytes 196612
  36.7 646.2 %copy-start.4 = (bf16[128,256]{1,0:T(8,128)(2,1)S(1)}, bf16[128,256]{1,0:T(8,128)(2,1)}, u32[]{:S(2)}) copy-start(bf16[128,256]{1,0:T(8,128)(2,1)} %param.9) | copy-start | bytes 196612
  44.0 663.9 %copy-start.3 = (s32[1,1,32]{2,1,0:T(1,128)S(1)}, s32[1,1,32]{2,1,0:T(1,128)}, u32[]{:S(2)}) copy-start(s32[1,1,32]{2,1,0:T(1,128)} %param.12) | copy-start | bytes 388
  630.1 669.5 %all-gather.5.cloned.1.call-start = ((), (), s32[]{:S(2)}) async-start(), calls=%async_computation.3 | async-start | bytes 2113536 | tf_op jit(solution)/shard_map/all_gather | solution.py:95
  684.0 14.0 collective-permute-start.6
  688.3 11.0 collective-permute-start.7
  690.8 8.5 collective-permute-start.8
  694.7 6.5 collective-permute-start.9
  696.7 5.6 collective-permute-start.10
  698.0 9.2 collective-permute-start.11
  707.9 645.9 %all-reduce.8.cloned.1.call-start = ((), (), s32[]{:S(2)}) async-start(), calls=%async_computation.4 | async-start | bytes 262144 | tf_op jit(solution)/shard_map/psum | solution.py:96
  1302.4 1120.3 %all-reduce.6.cloned.1.call-start = ((), (), s32[]{:S(2)}) async-start(), calls=%async_computation.2 | async-start | bytes 524288 | tf_op jit(solution)/shard_map/psum | solution.py:85
Sparse Core Ops, SparseCore 0:
  32.9 594.3 all-gather.2
  630.8 51.0 all-reduce.3
  708.0 591.5 all-gather.4
  1302.6 51.0 all-reduce.7
  1357.1 1065.5 all-reduce.5
where the time goes:
time: 2430 us
  waiting for transfers between devices  2360 us (97%)
  starting transfers between devices  31.5 us (1%)
    psum x1, waiting for transfers between devices, per_device(): weight_grad = lax.psum(weight_term, 'node')  1070 us
    all_gather x1, waiting for transfers between devices, per_device(): lax.all_gather(grad_piece, 'node', axis=0, tiled=True)  591 us
    all_gather x1, waiting for transfers between devices, per_device(): lax.all_gather(feature_piece, 'node', axis=0, tiled=True)  583 us
    psum x1, waiting for transfers between devices, per_device(): gathered, counted = lax.psum((partial_sum, degree_part), 'rep')  51.8 us
    psum x1, waiting for transfers between devices, per_device(): back_total = lax.psum(back_part, 'rep')  50.4 us
  transfers between devices with their start and end apart: 17, of which 11 were waited for; matrix products, arithmetic and copies ran while one was open for 0% of the time, Pallas kernels for 0%

commit v1 on v0

v1 whole, which is shorter than its diff:
```python
import jax
import jax.numpy as jnp
from jax import lax
from jax.experimental import pallas as pl
from jax.experimental.pallas import tpu as pltpu
from jax.sharding import Mesh, PartitionSpec as P

BF, F32, I32 = jnp.bfloat16, jnp.float32, jnp.int32
NODE, REP = ("z", "x", "yl"), ("yh", "c")
ROWS2, PLANE = ("x", "yl"), ("x", "yl", "yh", "c")
Z, K8, R4, PL = 16, 8, 4, 32
Q, W = 32, 256
PARAMS = pltpu.CompilerParams(vmem_limit_bytes=24 * 1024 * 1024)


def where_am_i():
    x = lax.axis_index("x")
    q = (x % 2) * 2 + lax.axis_index("yl")
    return x // 2, q, lax.axis_index("yh") * 2 + lax.axis_index("c")


def swap_pairs():
    pairs = []
    for x1 in range(2):
        for a in range(4):
            for b in range(4):
                pairs.append((x1 * 16 + a * 4 + b, x1 * 16 + b * 4 + a))
    return pairs


def call(body, shapes, *args):
    return pl.pallas_call(
        body,
        out_shape=shapes,
        in_specs=[pl.BlockSpec(memory_space=pltpu.VMEM)] * len(args),
        out_specs=jax.tree.map(lambda _: pl.BlockSpec(memory_space=pltpu.VMEM), shapes),
        compiler_params=PARAMS,
    )(*args)


def words_body(place_f, bits_f, place_b, bits_b, out):
    row = lax.broadcasted_iota(I32, (512, 512), 0)
    want = (((row // 4) % 16) * 2 + row // 256) * 16 + ((row // 64) % 4) * 4 + row % 4
    lane = lax.broadcasted_iota(I32, (32, 512), 1)
    spread = jnp.where(lane // 16 == lax.broadcasted_iota(I32, (32, 512), 0), 1.0, 0.0).astype(BF)
    column = lax.broadcasted_iota(I32, (8, 512), 1) % 16
    for half, (place, bits) in enumerate(((place_f, bits_f), (place_b, bits_b))):
        at = jnp.broadcast_to(place[...].astype(F32), (8, 32)).astype(BF)
        key = jnp.dot(at, spread, preferred_element_type=F32).astype(I32) * 16 + column
        hot = jnp.where(want == key[0:1, :], 1.0, 0.0).astype(BF)
        dense = jnp.dot(hot, bits[...].astype(F32).astype(BF), preferred_element_type=F32).astype(BF)
        for k in range(K8):
            out[k, half * 64 : half * 64 + 64, :] = dense[k * 64 : (k + 1) * 64]


def unpacked(words):
    spread = jnp.broadcast_to(words.astype(F32).astype(I32)[:, None, :], (64, 8, 128))
    bits = jnp.bitwise_and(jnp.right_shift(spread, lax.broadcasted_iota(I32, (64, 8, 128), 1)), 1)
    return bits.reshape(512, 128).astype(F32).astype(BF)


def over_columns(block, source):
    return lax.dot_general(block, source, (((0,), (0,)), ((), ())), preferred_element_type=F32)


def forward_body(words, gathered, out):
    source = gathered[...].reshape(Z * Q, W)
    upper = lax.broadcasted_iota(I32, (16, 512), 1) // 256
    ones = jnp.where(upper == lax.broadcasted_iota(I32, (16, 512), 0), 1.0, 0.0).astype(BF)
    for k in range(K8):
        block = unpacked(words[k, 0:64, :])
        part = over_columns(block, source).astype(BF)
        degree = jnp.dot(ones, block, preferred_element_type=F32).astype(BF)
        for q in range(4):
            dest = (k // 4) * 16 + q * 4 + k % 4
            out[dest, 0:32, :] = part[q * 32 : (q + 1) * 32]
            out[dest, 32:48, 0:128] = degree
            out[dest, 32:48, 128:256] = jnp.zeros_like(degree)


def middle_body(parts, own, weight, act, back, pushed, term):
    total = jnp.sum(parts[...].astype(F32), axis=0)
    x1, q, r = where_am_i()
    degree = total[32:33, 0:128] + total[33:34, 0:128]
    pick = lax.broadcasted_iota(I32, (32, 128), 1) == lax.broadcasted_iota(I32, (32, 128), 0) + q * 32
    counted = jnp.sum(jnp.where(pick, degree, 0.0), axis=1, keepdims=True)
    scaling = lax.rsqrt(1.0 + counted)
    hidden = (own[0:32, :].astype(F32) + total[0:32] * scaling).astype(BF)
    logits = jnp.dot(hidden, weight[...], preferred_element_type=F32)
    gate = jax.nn.sigmoid(logits)
    act[...] = (logits * gate).astype(BF)
    upstream = (own[32:64, :].astype(F32) * gate * (1.0 + logits * (1.0 - gate))).astype(BF)
    hidden_grad = lax.dot_general(
        upstream, weight[...], (((1,), (1,)), ((), ())), preferred_element_type=F32
    )
    back[...] = hidden_grad
    pushed[...] = (hidden_grad * scaling).astype(BF)
    term[...] = over_columns(hidden, upstream).astype(BF)


def two_parts(value):
    high = value.astype(BF).astype(F32)
    return jnp.concatenate([high, value - high], axis=0).astype(BF)


def send_body(terms, pushed, out):
    extra = two_parts(jnp.sum(terms[...].astype(F32), axis=0))
    for z in range(Z):
        out[z, 0:32, :] = pushed[...]
        out[z, 32:48, :] = extra


def backward_body(words, gathered, hidden_grad, out):
    x1, q, r = where_am_i()
    mine = (x1 * 4 + r) * 4 + q
    source = gathered[:, 0:32, :].reshape(Z * Q, W)
    slices = jnp.sum(gathered[:, 32:48, :].astype(F32), axis=0)
    extra = two_parts(slices[0:8] + slices[8:16])
    own = hidden_grad[...]
    for k in range(K8):
        part = over_columns(unpacked(words[k, 64:128, :]), source)
        for t in range(4):
            dest = k * 4 + t
            piece = part[t * 32 : (t + 1) * 32] + jnp.where(mine == dest, own, 0.0)
            out[dest, 0:32, :] = piece.astype(BF)
            out[dest, 32:48, :] = extra


def per_device(features, weight, out_grad, tile_place, tile_bits, back_place, back_bits):
    x1, q, r = where_am_i()
    quarter = jnp.concatenate(
        [lax.dynamic_slice_in_dim(a, r * Q, Q, 0) for a in (features, out_grad)], axis=0
    )
    own = lax.ppermute(quarter, PLANE, swap_pairs())
    words = call(
        words_body,
        jax.ShapeDtypeStruct((K8, 128, 128), BF),
        tile_place.reshape(1, 32),
        tile_bits.reshape(512, 128),
        back_place.reshape(1, 32),
        back_bits.reshape(512, 128),
    )
    words = lax.all_to_all(words, ROWS2, 0, 0)
    gathered = lax.all_to_all(jnp.broadcast_to(own[None, :Q], (Z, Q, W)), "z", 0, 0)
    parts = call(forward_body, jax.ShapeDtypeStruct((PL, 48, W), BF), words, gathered)
    parts = lax.all_to_all(parts, PLANE, 0, 0)
    act, hidden_grad, pushed, term = call(
        middle_body,
        (
            jax.ShapeDtypeStruct((Q, W), BF),
            jax.ShapeDtypeStruct((Q, W), F32),
            jax.ShapeDtypeStruct((Q, W), BF),
            jax.ShapeDtypeStruct((W, W), BF),
        ),
        parts,
        own,
        weight,
    )
    act = lax.ppermute(act, PLANE, swap_pairs())
    terms = lax.all_to_all(term.reshape(PL, 8, W), PLANE, 0, 0)
    sent = call(send_body, jax.ShapeDtypeStruct((Z, 48, W), BF), terms, pushed)
    gathered = lax.all_to_all(sent, "z", 0, 0)
    parts = call(
        backward_body, jax.ShapeDtypeStruct((PL, 48, W), BF), words, gathered, hidden_grad
    )
    parts = lax.all_to_all(parts, PLANE, 0, 0)
    input_grad = jnp.sum(parts[:, 0:32].astype(F32), axis=0).astype(BF)
    slices = parts[:, 32:48].astype(F32)
    weight_grad = (slices[:, 0:8] + slices[:, 8:16]).reshape(W, W)
    both = lax.all_gather(jnp.concatenate([act, input_grad], axis=0), REP, axis=0)
    return both[:, :Q].reshape(4 * Q, W), weight_grad, both[:, Q:].reshape(4 * Q, W)


def solution(mesh):
    fine = Mesh(mesh.devices.reshape(16, 4, 2, 2, 2), ("z", "x", "yl", "yh", "c"))
    return jax.shard_map(
        per_device,
        mesh=fine,
        in_specs=(
            P(NODE, None),
            P(),
            P(NODE, None),
            P(NODE, REP, None),
            P(NODE, REP, None, None, None),
            P(NODE, REP, None),
            P(NODE, REP, None, None, None),
        ),
        out_specs=(P(NODE, None), P(), P(NODE, None)),
        check_vma=False,
    )
```

time: 2430 us -> 144 us (0.06)
  the two profiles are of different devices: /device:TPU:24 before, /device:TPU:1 now
where the time goes in v1:
time: 144 us
  blocking collectives  92.9 us (65%)
  starting transfers between devices  28.3 us (20%)
  waiting for transfers between devices  12.8 us (9%)
  Pallas kernels  4.13 us (3%)
  local copies, waits for them, and re-layouts  3.98 us (3%)
    all_to_all x1, blocking collectives, per_device(): parts = lax.all_to_all(parts, PLANE, 0, 0)  26.9 us
    all_to_all x1, blocking collectives, per_device(): lax.all_to_all(jnp.broadcast_to(own[None, :Q], (Z, Q, W)), 'z', 0, 0)  25.2 us
    all_to_all x1, blocking collectives, per_device(): gathered = lax.all_to_all(sent, 'z', 0, 0)  22.6 us
    all_to_all x1, blocking collectives, per_device(): terms = lax.all_to_all(term.reshape(PL, 8, W), PLANE, 0, 0)  11.5 us
    all_to_all x1, starting transfers between devices, per_device(): parts = lax.all_to_all(parts, PLANE, 0, 0)  11 us
    all_to_all x1, waiting for transfers between devices, per_device(): parts = lax.all_to_all(parts, PLANE, 0, 0)  10.5 us
    ppermute x1, starting transfers between devices, per_device(): own = lax.ppermute(quarter, PLANE, swap_pairs())  7.86 us
    all_gather x1, blocking collectives, per_device(): lax.all_gather(jnp.concatenate([act, input_grad], axis=0), REP, axis=0)  6.79 us
  transfers between devices with their start and end apart: 4, of which 2 were waited for; matrix products, arithmetic and copies ran while one was open for 1% of the time, Pallas kernels for 0%

profile of v1, /device:TPU:1, one launch (start us, length us, event | category | flops | bytes accessed | tf_op | source)
XLA Modules:
  0.0 143.8 jit_solution(9869349465477781109)
XLA Ops:
  0.6 0.0 copy-start.3
  0.6 0.0 copy-start.4
  0.7 0.6 copy-done.3
  1.3 0.0 copy-done.4
  1.3 0.0 copy-start
  1.3 0.9 copy-done
  2.3 0.0 copy-start.1
  2.3 0.9 copy-done.1
  3.2 1.3 shard_map.94
  4.5 5.9 %all-to-all-start = ((bf16[8,128,128]{2,1,0:T(8,128)(2,1)}), bf16[8,128,128]{2,1,0:T(8,128)(2,1)S(1)}, u32[]{:S(2)}, u32[]{:S(2)}) async-start(bf16[8,128,128]{2,1,0:T(8,128)(2,1)} %shard_map.94), calls=%async_computation | async-start | bytes 524288 | tf_op jit(solution)/shard_map/all_to_all | solution.py:143
  10.3 0.7 constant_dynamic-slice_fusion
  11.1 7.9 %collective-permute-start = (bf16[64,256]{1,0:T(8,128)(2,1)S(1)}, bf16[64,256]{1,0:T(8,128)(2,1)S(1)}, u32[]{:S(2)}, u32[]{:S(2)}) collective-permute-start(bf16[64,256]{1,0:T(8,128)(2,1)S(1)} %pad_maximum_fusion), channel_id=1, source_target_pairs={{0,0},{1,4},{2,8},{3,12},{4,1},{5,5},{6,9},{7,13},{8,2},{9,6},{10,... | collective-permute-start | bytes 98312 | tf_op jit(solution)/shard_map/ppermute | solution.py:134
  18.9 2.3 %collective-permute-done.own = bf16[64,256]{1,0:T(8,128)(2,1)S(1)} collective-permute-done((bf16[64,256]{1,0:T(8,128)(2,1)S(1)}, bf16[64,256]{1,0:T(8,128)(2,1)S(1)}, u32[]{:S(2)}, u32[]{:S(2)}) %collective-permute-start) | collective-permute-done | bytes 32800 | tf_op jit(solution)/shard_map/ppermute | solution.py:134
  21.2 0.0 all-to-all-done.words
  21.3 25.2 %all_to_all.30.gathered = bf16[16,32,256]{2,1,0:T(8,128)(2,1)S(1)} all-to-all(bf16[16,32,256]{2,1,0:T(8,128)(2,1)S(1)} %broadcast_in_dim.2), channel_id=1, replica_groups=mesh['z'=16,'x'=4,'yl'=2,'yh'=2,'c'=2] {'z'}, dimensions={0} | all-to-all | bytes 524288 | tf_op jit(solution)/shard_map/all_to_all | solution.py:144
  46.5 0.7 shard_map.95
  47.2 0.0 copy-start.2
  47.2 26.9 %all_to_all.31.parts = bf16[32,48,256]{2,1,0:T(8,128)(2,1)S(1)} all-to-all(bf16[32,48,256]{2,1,0:T(8,128)(2,1)S(1)} %shard_map.95), channel_id=1, replica_groups=mesh['z'=16,'x'=4,'yl'=2,'yh'=2,'c'=2] {'x','yl','yh','c'}, dimensions={0} | all-to-all | bytes 1572864 | tf_op jit(solution)/shard_map/all_to_all | solution.py:146
  74.1 0.0 copy-done.2
  74.1 0.4 shard_map.96
  74.5 11.5 %all_to_all.32.terms = bf16[32,8,256]{2,1,0:T(8,128)(2,1)S(1)} all-to-all(bf16[32,8,256]{2,1,0:T(8,128)(2,1)S(1)} %bitcast.12), channel_id=1, replica_groups=mesh['z'=16,'x'=4,'yl'=2,'yh'=2,'c'=2] {'x','yl','yh','c'}, dimensions={0} | all-to-all | bytes 262144 | tf_op jit(solution)/shard_map/all_to_all | solution.py:160
  86.0 22.6 %all_to_all.33.gathered = bf16[16,48,256]{2,1,0:T(8,128)(2,1)S(1)} all-to-all(bf16[16,48,256]{2,1,0:T(8,128)(2,1)S(1)} %shard_map.97), channel_id=1, replica_groups=mesh['z'=16,'x'=4,'yl'=2,'yh'=2,'c'=2] {'z'}, dimensions={0} | all-to-all | bytes 786432 | tf_op jit(solution)/shard_map/all_to_all | solution.py:162
  108.6 1.7 %shard_map.98 = bf16[32,48,256]{2,1,0:T(8,128)(2,1)} custom-call(bf16[8,128,128]{2,1,0:T(8,128)(2,1)S(1)} %all-to-all-done.words, bf16[16,48,256]{2,1,0:T(8,128)(2,1)S(1)} %all_to_all.33.gathered, f32[32,256]{1,0:T(8,128)S(1)} %get-tuple-element.10.hidden_grad), custom_call_target="tpu_custom_call" | custom-call | tf_op jit(solution)/shard_map/pallas_call | solution.py:32
  110.3 11.0 %all-to-all-start.5 = ((bf16[32,48,256]{2,1,0:T(8,128)(2,1)}), bf16[32,48,256]{2,1,0:T(8,128)(2,1)S(1)}, u32[]{:S(2)}, u32[]{:S(2)}) async-start(bf16[32,48,256]{2,1,0:T(8,128)(2,1)} %shard_map.98), calls=%async_computation.5 | async-start | bytes 1572864 | tf_op jit(solution)/shard_map/all_to_all | solution.py:166
  121.3 3.6 %collective-permute-start.1 = (bf16[32,256]{1,0:T(8,128)(2,1)S(1)}, bf16[32,256]{1,0:T(8,128)(2,1)S(1)}, u32[]{:S(2)}, u32[]{:S(2)}) collective-permute-start(bf16[32,256]{1,0:T(8,128)(2,1)S(1)} %get-tuple-element.7), channel_id=1, source_target_pairs={{0,0},{1,4},{2,8},{3,12},{4,1},{5,5},{6,9},{7,13},{8,2},{9,6},{10,... | collective-permute-start | bytes 49160 | tf_op jit(solution)/shard_map/ppermute | solution.py:159
  124.9 10.5 %all-to-all-done.5 = bf16[32,48,256]{2,1,0:T(8,128)(2,1)S(1)} async-done(((bf16[32,48,256]{2,1,0:T(8,128)(2,1)}), bf16[32,48,256]{2,1,0:T(8,128)(2,1)S(1)}, u32[]{:S(2)}, u32[]{:S(2)}) %all-to-all-start.5) | async-done | bytes 786464 | tf_op jit(solution)/shard_map/all_to_all | solution.py:166
  135.5 0.7 fusion
  136.2 0.1 slice_reduce_fusion
  136.3 0.0 collective-permute-done.1
  136.3 6.8 %all-gather = bf16[256,256]{1,0:T(8,128)(2,1)S(1)} all-gather(bf16[64,256]{1,0:T(8,128)(2,1)S(1)} %pad_maximum_fusion.1), channel_id=2, replica_groups=mesh['z'=16,'x'=4,'yl'=2,'yh'=2,'c'=2] {'yh','c'}, dimensions={0}, use_global_device_ids=true | all-gather | bytes 163840 | tf_op jit(solution)/shard_map/all_gather | solution.py:170
  143.1 0.7 fusion.1
  (6 shorter events, 0.1 us)
Async XLA Ops:
  0.6 0.7 copy-start.3
  0.6 0.7 copy-start.4
  1.3 0.9 copy-start
  2.3 0.9 copy-start.1
  4.5 16.8 %all-to-all-start = ((bf16[8,128,128]{2,1,0:T(8,128)(2,1)}), bf16[8,128,128]{2,1,0:T(8,128)(2,1)S(1)}, u32[]{:S(2)}, u32[]{:S(2)}) async-start(bf16[8,128,128]{2,1,0:T(8,128)(2,1)} %shard_map.94), calls=%async_computation | async-start | bytes 524288 | tf_op jit(solution)/shard_map/all_to_all | solution.py:143
  11.1 10.2 %collective-permute-start = (bf16[64,256]{1,0:T(8,128)(2,1)S(1)}, bf16[64,256]{1,0:T(8,128)(2,1)S(1)}, u32[]{:S(2)}, u32[]{:S(2)}) collective-permute-start(bf16[64,256]{1,0:T(8,128)(2,1)S(1)} %pad_maximum_fusion), channel_id=1, source_target_pairs={{0,0},{1,4},{2,8},{3,12},{4,1},{5,5},{6,9},{7,13},{8,2},{9,6},{10,... | collective-permute-start | bytes 98312 | tf_op jit(solution)/shard_map/ppermute | solution.py:134
  47.2 26.9 %copy-start.2 = (bf16[256,256]{1,0:T(8,128)(2,1)S(1)}, bf16[256,256]{1,0:T(8,128)(2,1)}, u32[]{:S(2)}) copy-start(bf16[256,256]{1,0:T(8,128)(2,1)} %weight.1) | copy-start | bytes 393220
  110.3 25.1 %all-to-all-start.5 = ((bf16[32,48,256]{2,1,0:T(8,128)(2,1)}), bf16[32,48,256]{2,1,0:T(8,128)(2,1)S(1)}, u32[]{:S(2)}, u32[]{:S(2)}) async-start(bf16[32,48,256]{2,1,0:T(8,128)(2,1)} %shard_map.98), calls=%async_computation.5 | async-start | bytes 1572864 | tf_op jit(solution)/shard_map/all_to_all | solution.py:166
  121.3 15.0 %collective-permute-start.1 = (bf16[32,256]{1,0:T(8,128)(2,1)S(1)}, bf16[32,256]{1,0:T(8,128)(2,1)S(1)}, u32[]{:S(2)}, u32[]{:S(2)}) collective-permute-start(bf16[32,256]{1,0:T(8,128)(2,1)S(1)} %get-tuple-element.7), channel_id=1, source_target_pairs={{0,0},{1,4},{2,8},{3,12},{4,1},{5,5},{6,9},{7,13},{8,2},{9,6},{10,... | collective-permute-start | bytes 49160 | tf_op jit(solution)/shard_map/ppermute | solution.py:159

commit v2 on v1

v2 whole, which is shorter than its diff:
```python
import jax
import jax.numpy as jnp
from jax import lax
from jax.experimental import pallas as pl
from jax.experimental.pallas import tpu as pltpu
from jax.sharding import Mesh, PartitionSpec as P

BF, F32, I32 = jnp.bfloat16, jnp.float32, jnp.int32
NODE, REP = ("z", "x", "yl"), ("yh", "c")
ROWS2, PLANE = ("x", "yl"), ("x", "yl", "yh", "c")
Z, K8, R4, PL = 16, 8, 4, 32
Q, W = 32, 256
PARAMS = pltpu.CompilerParams(vmem_limit_bytes=24 * 1024 * 1024)


def where_am_i():
    x = lax.axis_index("x")
    q = (x % 2) * 2 + lax.axis_index("yl")
    return x // 2, q, lax.axis_index("yh") * 2 + lax.axis_index("c")


def swap_pairs():
    pairs = []
    for x1 in range(2):
        for a in range(4):
            for b in range(4):
                pairs.append((x1 * 16 + a * 4 + b, x1 * 16 + b * 4 + a))
    return pairs


def call(body, shapes, *args):
    return pl.pallas_call(
        body,
        out_shape=shapes,
        in_specs=[pl.BlockSpec(memory_space=pltpu.VMEM)] * len(args),
        out_specs=jax.tree.map(lambda _: pl.BlockSpec(memory_space=pltpu.VMEM), shapes),
        compiler_params=PARAMS,
    )(*args)


def words_body(place, bits, features, out):
    row = lax.broadcasted_iota(I32, (512, 512), 0)
    want = (((row // 4) % 16) * 2 + row // 256) * 16 + ((row // 64) % 4) * 4 + row % 4
    lane = lax.broadcasted_iota(I32, (32, 512), 1)
    spread = jnp.where(lane // 16 == lax.broadcasted_iota(I32, (32, 512), 0), 1.0, 0.0).astype(BF)
    column = lax.broadcasted_iota(I32, (8, 512), 1) % 16
    at = jnp.broadcast_to(place[...].astype(F32), (8, 32)).astype(BF)
    key = jnp.dot(at, spread, preferred_element_type=F32).astype(I32) * 16 + column
    hot = jnp.where(want == key[0:1, :], 1.0, 0.0).astype(BF)
    dense = jnp.dot(hot, bits[...].astype(F32).astype(BF), preferred_element_type=F32).astype(BF)
    for k in range(K8):
        out[k, 0:32, 0:128] = dense[k * 64 : k * 64 + 32]
        out[k, 0:32, 128:256] = dense[k * 64 + 32 : k * 64 + 64]
        out[k, 32:160, :] = features[...]


def unpacked(words):
    halves = []
    for h in range(2):
        half = words[:, h * 128 : (h + 1) * 128].astype(F32).astype(I32)
        spread = jnp.broadcast_to(half[:, None, :], (32, 8, 128))
        bits = jnp.bitwise_and(jnp.right_shift(spread, lax.broadcasted_iota(I32, (32, 8, 128), 1)), 1)
        halves.append(bits.reshape(256, 128).astype(F32).astype(BF))
    return jnp.concatenate(halves, axis=0)


def over_rows(block, source):
    return lax.dot_general(block, source, (((0,), (0,)), ((), ())), preferred_element_type=F32)


def forward_body(plane, out):
    block = jnp.concatenate([unpacked(plane[k, 0:32, :]) for k in range(K8)], axis=1)
    source = plane[:, 32:160, :].reshape(K8 * 128, W)
    part = jnp.dot(block, source, preferred_element_type=F32)
    fourth = lax.broadcasted_iota(I32, (16, 1024), 1) // 256
    ones = jnp.where(fourth == lax.broadcasted_iota(I32, (16, 1024), 0), 1.0, 0.0).astype(BF)
    degree = lax.dot_general(ones, block, (((1,), (1,)), ((), ())), preferred_element_type=F32)
    for z in range(Z):
        lanes = degree[0:8, (z // 4) * 128 : (z // 4 + 1) * 128]
        tail = jnp.concatenate([lanes, jnp.zeros_like(lanes)], axis=1)
        out[z] = jnp.concatenate([part[z * 32 : (z + 1) * 32], tail], axis=0).astype(BF)


def middle_body(parts, own, weight, act, back, pushed, term):
    total = jnp.sum(parts[...].astype(F32), axis=0)
    degree = jnp.sum(total[32:36, 0:128], axis=0, keepdims=True)
    first = (lax.axis_index("z") % 4) * 32
    pick = lax.broadcasted_iota(I32, (32, 128), 1) == lax.broadcasted_iota(I32, (32, 128), 0) + first
    counted = jnp.sum(jnp.where(pick, degree, 0.0), axis=1, keepdims=True)
    scaling = lax.rsqrt(1.0 + counted)
    hidden = (own[0:32, :].astype(F32) + total[0:32] * scaling).astype(BF)
    logits = jnp.dot(hidden, weight[...], preferred_element_type=F32)
    gate = jax.nn.sigmoid(logits)
    act[...] = (logits * gate).astype(BF)
    upstream = (own[32:64, :].astype(F32) * gate * (1.0 + logits * (1.0 - gate))).astype(BF)
    hidden_grad = lax.dot_general(
        upstream, weight[...], (((1,), (1,)), ((), ())), preferred_element_type=F32
    )
    back[...] = hidden_grad
    pushed[...] = (hidden_grad * scaling).astype(BF)
    term[...] = over_rows(hidden, upstream).astype(BF)


def two_parts(value):
    high = value.astype(BF).astype(F32)
    return jnp.concatenate([high, value - high], axis=0).astype(BF)


def send_body(terms, pushed, out):
    extra = jnp.sum(terms[...].astype(F32), axis=0)
    message = jnp.concatenate([pushed[...].astype(F32), extra], axis=0).astype(BF)
    for z in range(Z):
        out[z] = message


def backward_body(plane, gathered, hidden_grad, out):
    x1, q, r = where_am_i()
    mine = (x1 * 4 + r) * 4 + q
    received = gathered[...].astype(F32)
    source = received[:, 0:32].reshape(Z * Q, W).astype(BF)
    extra = two_parts(jnp.sum(received[:, 32:40], axis=0))
    own = hidden_grad[...]
    for k in range(K8):
        part = over_rows(unpacked(plane[k, 0:32, :]), source)
        for t in range(4):
            dest = k * 4 + t
            piece = part[t * 32 : (t + 1) * 32] + jnp.where(mine == dest, own, 0.0)
            out[dest, 0:32, :] = piece.astype(BF)
            out[dest, 32:48, :] = extra


def per_device(features, weight, out_grad, tile_place, tile_bits, back_place, back_bits):
    x1, q, r = where_am_i()
    quarter = jnp.concatenate(
        [lax.dynamic_slice_in_dim(a, r * Q, Q, 0) for a in (features, out_grad)], axis=0
    )
    own = lax.ppermute(quarter, PLANE, swap_pairs())
    plane = call(
        words_body,
        jax.ShapeDtypeStruct((K8, 160, W), BF),
        back_place.reshape(1, 32),
        back_bits.reshape(512, 128),
        features,
    )
    plane = lax.all_to_all(plane, ROWS2, 0, 0)
    parts = call(forward_body, jax.ShapeDtypeStruct((Z, 40, W), BF), plane)
    parts = lax.all_to_all(parts, "z", 0, 0)
    act, hidden_grad, pushed, term = call(
        middle_body,
        (
            jax.ShapeDtypeStruct((Q, W), BF),
            jax.ShapeDtypeStruct((Q, W), F32),
            jax.ShapeDtypeStruct((Q, W), BF),
            jax.ShapeDtypeStruct((W, W), BF),
        ),
        parts,
        own,
        weight,
    )
    act = lax.ppermute(act, PLANE, swap_pairs())
    terms = lax.all_to_all(term.reshape(PL, 8, W), PLANE, 0, 0)
    sent = call(send_body, jax.ShapeDtypeStruct((Z, 40, W), BF), terms, pushed)
    gathered = lax.all_to_all(sent, "z", 0, 0)
    parts = call(
        backward_body, jax.ShapeDtypeStruct((PL, 48, W), BF), plane, gathered, hidden_grad
    )
    parts = lax.all_to_all(parts, PLANE, 0, 0)
    input_grad = jnp.sum(parts[:, 0:32].astype(F32), axis=0).astype(BF)
    slices = parts[:, 32:48].astype(F32)
    weight_grad = (slices[:, 0:8] + slices[:, 8:16]).reshape(W, W)
    both = lax.all_gather(jnp.concatenate([act, input_grad], axis=0), REP, axis=0)
    return both[:, :Q].reshape(4 * Q, W), weight_grad, both[:, Q:].reshape(4 * Q, W)


def solution(mesh):
    fine = Mesh(mesh.devices.reshape(16, 4, 2, 2, 2), ("z", "x", "yl", "yh", "c"))
    return jax.shard_map(
        per_device,
        mesh=fine,
        in_specs=(
            P(NODE, None),
            P(),
            P(NODE, None),
            P(NODE, REP, None),
            P(NODE, REP, None, None, None),
            P(NODE, REP, None),
            P(NODE, REP, None, None, None),
        ),
        out_specs=(P(NODE, None), P(), P(NODE, None)),
        check_vma=False,
    )
```

time: 144 us -> 126 us (0.88)
  blocking collectives: 92.9 us -> 62.4 us
  starting transfers between devices: 28.3 us -> 35.9 us
  waiting for transfers between devices: 12.8 us -> 18.1 us
    all_to_all x2 -> x1, blocking collectives: 52.1 us -> 13.7 us  [per_device(): plane = lax.all_to_all(plane, ROWS2, 0, 0)]
    all_to_all x1, starting transfers between devices: 5.86 us -> 16.8 us  [per_device(): parts = lax.all_to_all(parts, 'z', 0, 0)]
    all_to_all x1, blocking collectives: 11.5 us -> 21.2 us  [per_device(): terms = lax.all_to_all(term.reshape(PL, 8, W), PLANE, 0, 0)]
    all_to_all x1, waiting for transfers between devices: 0.01 us -> 6.05 us  [per_device(): parts = lax.all_to_all(parts, 'z', 0, 0)]
    ppermute x1, starting transfers between devices: 7.86 us -> 5.08 us  [per_device(): own = lax.ppermute(quarter, PLANE, swap_pairs())]
    all_to_all x1, blocking collectives: 22.6 us -> 20.6 us  [per_device(): gathered = lax.all_to_all(sent, 'z', 0, 0)]
  transfers between devices with their start and end apart: 4 -> 4, of which waited for: 2 -> 3; matrix products, arithmetic and copies ran while one was open for 1% -> 1% of each run, Pallas kernels for 0% -> 0%
where the time goes in v2:
time: 126 us
  blocking collectives  62.4 us (50%)
  starting transfers between devices  35.9 us (28%)
  waiting for transfers between devices  18.1 us (14%)
  Pallas kernels  4.01 us (3%)
  local copies, waits for them, and re-layouts  3.9 us (3%)
    all_to_all x1, blocking collectives, per_device(): terms = lax.all_to_all(term.reshape(PL, 8, W), PLANE, 0, 0)  21.2 us
    all_to_all x1, blocking collectives, per_device(): gathered = lax.all_to_all(sent, 'z', 0, 0)  20.6 us
    all_to_all x1, starting transfers between devices, per_device(): parts = lax.all_to_all(parts, 'z', 0, 0)  16.8 us
    all_to_all x1, blocking collectives, per_device(): plane = lax.all_to_all(plane, ROWS2, 0, 0)  13.7 us
    all_to_all x1, waiting for transfers between devices, per_device(): parts = lax.all_to_all(parts, PLANE, 0, 0)  10.5 us
    all_to_all x1, starting transfers between devices, per_device(): parts = lax.all_to_all(parts, PLANE, 0, 0)  10.4 us
    all_gather x1, blocking collectives, per_device(): lax.all_gather(jnp.concatenate([act, input_grad], axis=0), REP, axis=0)  6.79 us
    all_to_all x1, waiting for transfers between devices, per_device(): parts = lax.all_to_all(parts, 'z', 0, 0)  6.05 us
  transfers between devices with their start and end apart: 4, of which 3 were waited for; matrix products, arithmetic and copies ran while one was open for 1% of the time, Pallas kernels for 0%

profile of v2, /device:TPU:1, one launch (start us, length us, event | category | flops | bytes accessed | tf_op | source)
XLA Modules:
  0.0 125.9 jit_solution(15252071436607577649)
XLA Ops:
  0.6 0.0 copy-start
  0.6 0.0 copy-start.4
  0.7 0.7 copy-done.4
  1.3 0.0 copy-start.1
  1.3 0.9 copy-done.1
  2.3 0.0 copy-start.3
  2.3 0.8 copy-done.3
  3.1 0.4 shard_map.76
  3.5 13.7 %all_to_all.25.plane = bf16[8,160,256]{2,1,0:T(8,128)(2,1)S(1)} all-to-all(bf16[8,160,256]{2,1,0:T(8,128)(2,1)S(1)} %shard_map.76), channel_id=1, replica_groups=mesh['z'=16,'x'=4,'yl'=2,'yh'=2,'c'=2] {'x','yl'}, dimensions={0} | all-to-all | bytes 1310720 | tf_op jit(solution)/shard_map/all_to_all | solution.py:145
  17.3 1.5 %shard_map.77 = bf16[16,40,256]{2,1,0:T(8,128)(2,1)} custom-call(bf16[8,160,256]{2,1,0:T(8,128)(2,1)S(1)} %all_to_all.25.plane), custom_call_target="tpu_custom_call" | custom-call | tf_op jit(solution)/shard_map/pallas_call | solution.py:32
  18.8 16.8 %all-to-all-start.1 = ((bf16[16,40,256]{2,1,0:T(8,128)(2,1)}), bf16[16,40,256]{2,1,0:T(8,128)(2,1)S(1)}, u32[]{:S(2)}, u32[]{:S(2)}) async-start(bf16[16,40,256]{2,1,0:T(8,128)(2,1)} %shard_map.77), calls=%async_computation.1 | async-start | bytes 655360 | tf_op jit(solution)/shard_map/all_to_all | solution.py:147
  35.6 0.0 copy-start.2
  35.6 0.8 constant_dynamic-slice_fusion.1
  36.4 0.0 copy-done
  36.4 5.1 %collective-permute-start = (bf16[64,256]{1,0:T(8,128)(2,1)S(1)}, bf16[64,256]{1,0:T(8,128)(2,1)S(1)}, u32[]{:S(2)}, u32[]{:S(2)}) collective-permute-start(bf16[64,256]{1,0:T(8,128)(2,1)S(1)} %pad_maximum_fusion), channel_id=1, source_target_pairs={{0,0},{1,4},{2,8},{3,12},{4,1},{5,5},{6,9},{7,13},{8,2},{9,6},{10,... | collective-permute-start | bytes 98312 | tf_op jit(solution)/shard_map/ppermute | solution.py:137
  41.5 1.6 %collective-permute-done.own = bf16[64,256]{1,0:T(8,128)(2,1)S(1)} collective-permute-done((bf16[64,256]{1,0:T(8,128)(2,1)S(1)}, bf16[64,256]{1,0:T(8,128)(2,1)S(1)}, u32[]{:S(2)}, u32[]{:S(2)}) %collective-permute-start) | collective-permute-done | bytes 32800 | tf_op jit(solution)/shard_map/ppermute | solution.py:137
  43.1 6.1 %all-to-all-done.1.parts = bf16[16,40,256]{2,1,0:T(8,128)(2,1)S(1)} async-done(((bf16[16,40,256]{2,1,0:T(8,128)(2,1)}), bf16[16,40,256]{2,1,0:T(8,128)(2,1)S(1)}, u32[]{:S(2)}, u32[]{:S(2)}) %all-to-all-start.1) | async-done | bytes 327712 | tf_op jit(solution)/shard_map/all_to_all | solution.py:147
  49.1 0.0 copy-done.2
  49.1 0.4 shard_map.78
  49.6 21.2 %all_to_all.26.terms = bf16[32,8,256]{2,1,0:T(8,128)(2,1)S(1)} all-to-all(bf16[32,8,256]{2,1,0:T(8,128)(2,1)S(1)} %bitcast.9), channel_id=1, replica_groups=mesh['z'=16,'x'=4,'yl'=2,'yh'=2,'c'=2] {'x','yl','yh','c'}, dimensions={0} | all-to-all | bytes 262144 | tf_op jit(solution)/shard_map/all_to_all | solution.py:161
  70.8 20.6 %all_to_all.27.gathered = bf16[16,40,256]{2,1,0:T(8,128)(2,1)S(1)} all-to-all(bf16[16,40,256]{2,1,0:T(8,128)(2,1)S(1)} %shard_map.79), channel_id=1, replica_groups=mesh['z'=16,'x'=4,'yl'=2,'yh'=2,'c'=2] {'z'}, dimensions={0} | all-to-all | bytes 655360 | tf_op jit(solution)/shard_map/all_to_all | solution.py:163
  91.4 1.7 %shard_map.80 = bf16[32,48,256]{2,1,0:T(8,128)(2,1)} custom-call(bf16[8,160,256]{2,1,0:T(8,128)(2,1)S(1)} %all_to_all.25.plane, bf16[16,40,256]{2,1,0:T(8,128)(2,1)S(1)} %all_to_all.27.gathered, f32[32,256]{1,0:T(8,128)S(1)} %get-tuple-element.10.hidden_grad), custom_call_target="tpu_custom_call" | custom-call | tf_op jit(solution)/shard_map/pallas_call | solution.py:32
  93.1 10.4 %all-to-all-start.4 = ((bf16[32,48,256]{2,1,0:T(8,128)(2,1)}), bf16[32,48,256]{2,1,0:T(8,128)(2,1)S(1)}, u32[]{:S(2)}, u32[]{:S(2)}) async-start(bf16[32,48,256]{2,1,0:T(8,128)(2,1)} %shard_map.80), calls=%async_computation.4 | async-start | bytes 1572864 | tf_op jit(solution)/shard_map/all_to_all | solution.py:167
  103.5 3.5 %collective-permute-start.1 = (bf16[32,256]{1,0:T(8,128)(2,1)S(1)}, bf16[32,256]{1,0:T(8,128)(2,1)S(1)}, u32[]{:S(2)}, u32[]{:S(2)}) collective-permute-start(bf16[32,256]{1,0:T(8,128)(2,1)S(1)} %get-tuple-element.7), channel_id=1, source_target_pairs={{0,0},{1,4},{2,8},{3,12},{4,1},{5,5},{6,9},{7,13},{8,2},{9,6},{10,... | collective-permute-start | bytes 49160 | tf_op jit(solution)/shard_map/ppermute | solution.py:160
  107.1 10.5 %all-to-all-done.4 = bf16[32,48,256]{2,1,0:T(8,128)(2,1)S(1)} async-done(((bf16[32,48,256]{2,1,0:T(8,128)(2,1)}), bf16[32,48,256]{2,1,0:T(8,128)(2,1)S(1)}, u32[]{:S(2)}, u32[]{:S(2)}) %all-to-all-start.4) | async-done | bytes 786464 | tf_op jit(solution)/shard_map/all_to_all | solution.py:167
  117.6 0.7 fusion
  118.4 0.1 slice_reduce_fusion
  118.5 0.0 collective-permute-done.1
  118.5 6.8 %all-gather = bf16[256,256]{1,0:T(8,128)(2,1)S(1)} all-gather(bf16[64,256]{1,0:T(8,128)(2,1)S(1)} %pad_maximum_fusion.1), channel_id=2, replica_groups=mesh['z'=16,'x'=4,'yl'=2,'yh'=2,'c'=2] {'yh','c'}, dimensions={0}, use_global_device_ids=true | all-gather | bytes 163840 | tf_op jit(solution)/shard_map/all_gather | solution.py:171
  125.3 0.7 fusion.1
  (5 shorter events, 0.1 us)
Async XLA Ops:
  0.6 35.8 %copy-start = (bf16[128,256]{1,0:T(8,128)(2,1)S(1)}, bf16[128,256]{1,0:T(8,128)(2,1)}, u32[]{:S(2)}) copy-start(bf16[128,256]{1,0:T(8,128)(2,1)} %param.9) | copy-start | bytes 196612
  0.6 0.7 copy-start.4
  1.3 0.9 copy-start.1
  2.3 0.8 copy-start.3
  18.8 30.4 %all-to-all-start.1 = ((bf16[16,40,256]{2,1,0:T(8,128)(2,1)}), bf16[16,40,256]{2,1,0:T(8,128)(2,1)S(1)}, u32[]{:S(2)}, u32[]{:S(2)}) async-start(bf16[16,40,256]{2,1,0:T(8,128)(2,1)} %shard_map.77), calls=%async_computation.1 | async-start | bytes 655360 | tf_op jit(solution)/shard_map/all_to_all | solution.py:147
  35.6 13.5 %copy-start.2 = (bf16[256,256]{1,0:T(8,128)(2,1)S(1)}, bf16[256,256]{1,0:T(8,128)(2,1)}, u32[]{:S(2)}) copy-start(bf16[256,256]{1,0:T(8,128)(2,1)} %weight.1) | copy-start | bytes 393220
  36.4 6.7 %collective-permute-start = (bf16[64,256]{1,0:T(8,128)(2,1)S(1)}, bf16[64,256]{1,0:T(8,128)(2,1)S(1)}, u32[]{:S(2)}, u32[]{:S(2)}) collective-permute-start(bf16[64,256]{1,0:T(8,128)(2,1)S(1)} %pad_maximum_fusion), channel_id=1, source_target_pairs={{0,0},{1,4},{2,8},{3,12},{4,1},{5,5},{6,9},{7,13},{8,2},{9,6},{10,... | collective-permute-start | bytes 98312 | tf_op jit(solution)/shard_map/ppermute | solution.py:137
  93.1 24.5 %all-to-all-start.4 = ((bf16[32,48,256]{2,1,0:T(8,128)(2,1)}), bf16[32,48,256]{2,1,0:T(8,128)(2,1)S(1)}, u32[]{:S(2)}, u32[]{:S(2)}) async-start(bf16[32,48,256]{2,1,0:T(8,128)(2,1)} %shard_map.80), calls=%async_computation.4 | async-start | bytes 1572864 | tf_op jit(solution)/shard_map/all_to_all | solution.py:167
  103.5 14.9 %collective-permute-start.1 = (bf16[32,256]{1,0:T(8,128)(2,1)S(1)}, bf16[32,256]{1,0:T(8,128)(2,1)S(1)}, u32[]{:S(2)}, u32[]{:S(2)}) collective-permute-start(bf16[32,256]{1,0:T(8,128)(2,1)S(1)} %get-tuple-element.7), channel_id=1, source_target_pairs={{0,0},{1,4},{2,8},{3,12},{4,1},{5,5},{6,9},{7,13},{8,2},{9,6},{10,... | collective-permute-start | bytes 49160 | tf_op jit(solution)/shard_map/ppermute | solution.py:160

commit v3 on v2

--- a/solution.py
+++ b/solution.py
@@ -38,7 +38,13 @@
     )(*args)
 
 
-def words_body(place, bits, features, out):
+def words_body(place, bits_far, features_far, out, bits, features, sems):
+    fetches = [
+        pltpu.make_async_copy(bits_far, bits, sems.at[0]),
+        pltpu.make_async_copy(features_far, features, sems.at[1]),
+    ]
+    for fetch in fetches:
+        fetch.start()
     row = lax.broadcasted_iota(I32, (512, 512), 0)
     want = (((row // 4) % 16) * 2 + row // 256) * 16 + ((row // 64) % 4) * 4 + row % 4
     lane = lax.broadcasted_iota(I32, (32, 512), 1)
@@ -47,6 +53,8 @@
     at = jnp.broadcast_to(place[...].astype(F32), (8, 32)).astype(BF)
     key = jnp.dot(at, spread, preferred_element_type=F32).astype(I32) * 16 + column
     hot = jnp.where(want == key[0:1, :], 1.0, 0.0).astype(BF)
+    for fetch in fetches:
+        fetch.wait()
     dense = jnp.dot(hot, bits[...].astype(F32).astype(BF), preferred_element_type=F32).astype(BF)
     for k in range(K8):
         out[k, 0:32, 0:128] = dense[k * 64 : k * 64 + 32]
@@ -113,20 +121,34 @@
         out[z] = message
 
 
-def backward_body(plane, gathered, hidden_grad, out):
+def backward_body(plane, gathered, hidden_grad, out, total):
     x1, q, r = where_am_i()
-    mine = (x1 * 4 + r) * 4 + q
     received = gathered[...].astype(F32)
     source = received[:, 0:32].reshape(Z * Q, W).astype(BF)
     extra = two_parts(jnp.sum(received[:, 32:40], axis=0))
-    own = hidden_grad[...]
-    for k in range(K8):
-        part = over_rows(unpacked(plane[k, 0:32, :]), source)
-        for t in range(4):
-            dest = k * 4 + t
-            piece = part[t * 32 : (t + 1) * 32] + jnp.where(mine == dest, own, 0.0)
-            out[dest, 0:32, :] = piece.astype(BF)
-            out[dest, 32:48, :] = extra
+    for k in range(K8):
+        total[k] = over_rows(unpacked(plane[k, 0:32, :]), source)
+    rows = pl.ds(pl.multiple_of(q * 32, 32), 32)
+    total[x1 * 4 + r, rows, :] = total[x1 * 4 + r, rows, :] + hidden_grad[...]
+    for k in range(K8):
+        out[k, 0:128, :] = total[k].astype(BF)
+        out[k, 128:144, :] = extra
+
+
+def share_body(parts, act, out):
+    out[0:128, :] = jnp.sum(parts[:, 0:128, :].astype(F32), axis=0).astype(BF)
+    for k in range(K8):
+        out[128 + k * 16 : 144 + k * 16, :] = parts[k, 128:144, :]
+    out[256:288, :] = act[...]
+
+
+def finish_body(shares, activation, weight_grad, input_grad):
+    input_grad[...] = jnp.sum(shares[:, 0:128, :].astype(F32), axis=0).astype(BF)
+    for r in range(R4):
+        activation[r * 32 : (r + 1) * 32, :] = shares[r, 256:288, :]
+        for k in range(K8):
+            both = shares[r, 128 + k * 16 : 144 + k * 16, :].astype(F32)
+            weight_grad[k * 32 + r * 8 : k * 32 + r * 8 + 8, :] = both[0:8] + both[8:16]
 
 
 def per_device(features, weight, out_grad, tile_place, tile_bits, back_place, back_bits):
@@ -135,13 +157,19 @@
         [lax.dynamic_slice_in_dim(a, r * Q, Q, 0) for a in (features, out_grad)], axis=0
     )
     own = lax.ppermute(quarter, PLANE, swap_pairs())
-    plane = call(
+    near, far = pl.BlockSpec(memory_space=pltpu.VMEM), pl.BlockSpec(memory_space=pl.ANY)
+    plane = pl.pallas_call(
         words_body,
-        jax.ShapeDtypeStruct((K8, 160, W), BF),
-        back_place.reshape(1, 32),
-        back_bits.reshape(512, 128),
-        features,
-    )
+        out_shape=jax.ShapeDtypeStruct((K8, 160, W), BF),
+        in_specs=[near, far, far],
+        out_specs=near,
+        scratch_shapes=[
+            pltpu.VMEM((512, 128), I32),
+            pltpu.VMEM((128, W), BF),
+            pltpu.SemaphoreType.DMA((2,)),
+        ],
+        compiler_params=PARAMS,
+    )(back_place.reshape(1, 32), back_bits.reshape(512, 128), features)
     plane = lax.all_to_all(plane, ROWS2, 0, 0)
     parts = call(forward_body, jax.ShapeDtypeStruct((Z, 40, W), BF), plane)
     parts = lax.all_to_all(parts, "z", 0, 0)
@@ -161,15 +189,26 @@
     terms = lax.all_to_all(term.reshape(PL, 8, W), PLANE, 0, 0)
     sent = call(send_body, jax.ShapeDtypeStruct((Z, 40, W), BF), terms, pushed)
     gathered = lax.all_to_all(sent, "z", 0, 0)
-    parts = call(
-        backward_body, jax.ShapeDtypeStruct((PL, 48, W), BF), plane, gathered, hidden_grad
-    )
-    parts = lax.all_to_all(parts, PLANE, 0, 0)
-    input_grad = jnp.sum(parts[:, 0:32].astype(F32), axis=0).astype(BF)
-    slices = parts[:, 32:48].astype(F32)
-    weight_grad = (slices[:, 0:8] + slices[:, 8:16]).reshape(W, W)
-    both = lax.all_gather(jnp.concatenate([act, input_grad], axis=0), REP, axis=0)
-    return both[:, :Q].reshape(4 * Q, W), weight_grad, both[:, Q:].reshape(4 * Q, W)
+    parts = pl.pallas_call(
+        backward_body,
+        out_shape=jax.ShapeDtypeStruct((K8, 144, W), BF),
+        in_specs=[near] * 3,
+        out_specs=near,
+        scratch_shapes=[pltpu.VMEM((K8, 128, W), F32)],
+        compiler_params=PARAMS,
+    )(plane, gathered, hidden_grad)
+    parts = lax.all_to_all(parts, ROWS2, 0, 0)
+    share = call(share_body, jax.ShapeDtypeStruct((288, W), BF), parts, act)
+    shares = lax.all_gather(share, REP, axis=0)
+    return call(
+        finish_body,
+        (
+            jax.ShapeDtypeStruct((4 * Q, W), BF),
+            jax.ShapeDtypeStruct((W, W), F32),
+            jax.ShapeDtypeStruct((4 * Q, W), BF),
+        ),
+        shares,
+    )
 
 
 def solution(mesh):

time: 126 us -> 122 us (0.968)
  waiting for transfers between devices: 18.1 us -> 9.34 us
  blocking collectives: 62.4 us -> 67 us
    all_to_all x1, waiting for transfers between devices: 10.5 us -> 0.01 us  [per_device(): parts = lax.all_to_all(parts, ROWS2, 0, 0)]
    all_to_all x1, starting transfers between devices: 10.4 us -> 3.54 us  [per_device(): parts = lax.all_to_all(parts, ROWS2, 0, 0)]
    ppermute x1, starting transfers between devices: 3.54 us -> 10.2 us  [per_device(): act = lax.ppermute(act, PLANE, swap_pairs())]
    all_gather x1, blocking collectives: 6.79 us -> 11.4 us  [per_device(): shares = lax.all_gather(share, REP, axis=0)]
    pallas_call x0 -> x2, Pallas kernels: none -> 2.25 us  [the longest x1 1.63 us: per_device(): pl.pallas_call(backward_body, out_shape=jax.ShapeDtypeStruct((K8, 144, W)...]
    ppermute x1, waiting for transfers between devices: 0.01 us -> 1.7 us  [per_device(): act = lax.ppermute(act, PLANE, swap_pairs())]
where the time goes in v3:
time: 122 us; the launch traced here: 121 us
  blocking collectives  67 us (55%)
  starting transfers between devices  35.7 us (29%)
  waiting for transfers between devices  9.34 us (8%)
  Pallas kernels  5.01 us (4%)
  local copies, waits for them, and re-layouts  3.24 us (3%)
    all_to_all x1, blocking collectives, per_device(): terms = lax.all_to_all(term.reshape(PL, 8, W), PLANE, 0, 0)  21.2 us
    all_to_all x1, blocking collectives, per_device(): gathered = lax.all_to_all(sent, 'z', 0, 0)  20.6 us
    all_to_all x1, starting transfers between devices, per_device(): parts = lax.all_to_all(parts, 'z', 0, 0)  16.8 us
    all_to_all x1, blocking collectives, per_device(): plane = lax.all_to_all(plane, ROWS2, 0, 0)  13.7 us
    all_gather x1, blocking collectives, per_device(): shares = lax.all_gather(share, REP, axis=0)  11.4 us
    ppermute x1, starting transfers between devices, per_device(): act = lax.ppermute(act, PLANE, swap_pairs())  10.2 us
    all_to_all x1, waiting for transfers between devices, per_device(): parts = lax.all_to_all(parts, 'z', 0, 0)  6.05 us
    ppermute x1, starting transfers between devices, per_device(): own = lax.ppermute(quarter, PLANE, swap_pairs())  5.08 us
  transfers between devices with their start and end apart: 4, of which 3 were waited for; matrix products, arithmetic and copies ran while one was open for 1% of the time, Pallas kernels for 0%

profile of v3, /device:TPU:1, one launch (start us, length us, event | category | flops | bytes accessed | tf_op | source)
XLA Modules:
  0.0 121.0 jit_solution(14405394191978529052)
XLA Ops:
  0.6 0.0 copy-start
  0.6 0.0 copy-start.4
  0.7 0.7 copy-done.4
  1.3 0.0 copy-start.1
  1.3 0.9 copy-done.1
  2.3 0.0 copy-start.3
  2.3 0.8 copy-done.3
  3.1 0.6 shard_map.76
  3.8 13.7 %all_to_all.25.plane = bf16[8,160,256]{2,1,0:T(8,128)(2,1)S(1)} all-to-all(bf16[8,160,256]{2,1,0:T(8,128)(2,1)S(1)} %shard_map.76), channel_id=1, replica_groups=mesh['z'=16,'x'=4,'yl'=2,'yh'=2,'c'=2] {'x','yl'}, dimensions={0} | all-to-all | bytes 1310720 | tf_op jit(solution)/shard_map/all_to_all | solution.py:173
  17.5 1.5 %shard_map.77 = bf16[16,40,256]{2,1,0:T(8,128)(2,1)} custom-call(bf16[8,160,256]{2,1,0:T(8,128)(2,1)S(1)} %all_to_all.25.plane), custom_call_target="tpu_custom_call" | custom-call | tf_op jit(solution)/shard_map/pallas_call | solution.py:32
  19.0 16.8 %all-to-all-start.1 = ((bf16[16,40,256]{2,1,0:T(8,128)(2,1)}), bf16[16,40,256]{2,1,0:T(8,128)(2,1)S(1)}, u32[]{:S(2)}, u32[]{:S(2)}) async-start(bf16[16,40,256]{2,1,0:T(8,128)(2,1)} %shard_map.77), calls=%async_computation.1 | async-start | bytes 655360 | tf_op jit(solution)/shard_map/all_to_all | solution.py:175
  35.8 0.0 copy-start.2
  35.8 0.8 constant_dynamic-slice_fusion.1
  36.6 0.0 copy-done
  36.6 5.1 %collective-permute-start = (bf16[64,256]{1,0:T(8,128)(2,1)S(1)}, bf16[64,256]{1,0:T(8,128)(2,1)S(1)}, u32[]{:S(2)}, u32[]{:S(2)}) collective-permute-start(bf16[64,256]{1,0:T(8,128)(2,1)S(1)} %pad_maximum_fusion), channel_id=1, source_target_pairs={{0,0},{1,4},{2,8},{3,12},{4,1},{5,5},{6,9},{7,13},{8,2},{9,6},{10,... | collective-permute-start | bytes 98312 | tf_op jit(solution)/shard_map/ppermute | solution.py:159
  41.7 1.6 %collective-permute-done.own = bf16[64,256]{1,0:T(8,128)(2,1)S(1)} collective-permute-done((bf16[64,256]{1,0:T(8,128)(2,1)S(1)}, bf16[64,256]{1,0:T(8,128)(2,1)S(1)}, u32[]{:S(2)}, u32[]{:S(2)}) %collective-permute-start) | collective-permute-done | bytes 32800 | tf_op jit(solution)/shard_map/ppermute | solution.py:159
  43.3 6.1 %all-to-all-done.1.parts = bf16[16,40,256]{2,1,0:T(8,128)(2,1)S(1)} async-done(((bf16[16,40,256]{2,1,0:T(8,128)(2,1)}), bf16[16,40,256]{2,1,0:T(8,128)(2,1)S(1)}, u32[]{:S(2)}, u32[]{:S(2)}) %all-to-all-start.1) | async-done | bytes 327712 | tf_op jit(solution)/shard_map/all_to_all | solution.py:175
  49.3 0.0 copy-done.2
  49.3 0.4 shard_map.78
  49.8 21.2 %all_to_all.26.terms = bf16[32,8,256]{2,1,0:T(8,128)(2,1)S(1)} all-to-all(bf16[32,8,256]{2,1,0:T(8,128)(2,1)S(1)} %bitcast.6), channel_id=1, replica_groups=mesh['z'=16,'x'=4,'yl'=2,'yh'=2,'c'=2] {'x','yl','yh','c'}, dimensions={0} | all-to-all | bytes 262144 | tf_op jit(solution)/shard_map/all_to_all | solution.py:189
  71.0 20.6 %all_to_all.27.gathered = bf16[16,40,256]{2,1,0:T(8,128)(2,1)S(1)} all-to-all(bf16[16,40,256]{2,1,0:T(8,128)(2,1)S(1)} %shard_map.79), channel_id=1, replica_groups=mesh['z'=16,'x'=4,'yl'=2,'yh'=2,'c'=2] {'z'}, dimensions={0} | all-to-all | bytes 655360 | tf_op jit(solution)/shard_map/all_to_all | solution.py:191
  91.6 1.6 %shard_map.80 = bf16[8,144,256]{2,1,0:T(8,128)(2,1)} custom-call(bf16[8,160,256]{2,1,0:T(8,128)(2,1)S(1)} %all_to_all.25.plane, bf16[16,40,256]{2,1,0:T(8,128)(2,1)S(1)} %all_to_all.27.gathered, f32[32,256]{1,0:T(8,128)S(1)} %get-tuple-element.9.hidden_grad), custom_call_target="tpu_custom_call" | custom-call | tf_op jit(solution)/shard_map/pallas_call | solution.py:192
  93.3 3.5 %all-to-all-start.4 = ((bf16[8,144,256]{2,1,0:T(8,128)(2,1)}), bf16[8,144,256]{2,1,0:T(8,128)(2,1)S(1)}, u32[]{:S(2)}, u32[]{:S(2)}) async-start(bf16[8,144,256]{2,1,0:T(8,128)(2,1)} %shard_map.80), calls=%async_computation.4 | async-start | bytes 1179648 | tf_op jit(solution)/shard_map/all_to_all | solution.py:200
  96.8 10.2 %collective-permute-start.1 = (bf16[32,256]{1,0:T(8,128)(2,1)S(1)}, bf16[32,256]{1,0:T(8,128)(2,1)S(1)}, u32[]{:S(2)}, u32[]{:S(2)}) collective-permute-start(bf16[32,256]{1,0:T(8,128)(2,1)S(1)} %get-tuple-element.10), channel_id=1, source_target_pairs={{0,0},{1,4},{2,8},{3,12},{4,1},{5,5},{6,9},{7,13},{8,2},{9,6},{10,... | collective-permute-start | bytes 49160 | tf_op jit(solution)/shard_map/ppermute | solution.py:188
  107.1 1.7 %collective-permute-done.1.act = bf16[32,256]{1,0:T(8,128)(2,1)S(1)} collective-permute-done((bf16[32,256]{1,0:T(8,128)(2,1)S(1)}, bf16[32,256]{1,0:T(8,128)(2,1)S(1)}, u32[]{:S(2)}, u32[]{:S(2)}) %collective-permute-start.1) | collective-permute-done | bytes 16416 | tf_op jit(solution)/shard_map/ppermute | solution.py:188
  108.8 0.0 all-to-all-done.4.parts
  108.8 0.1 shard_map.81
  108.9 11.4 %all-gather = bf16[1152,256]{1,0:T(8,128)(2,1)S(1)} all-gather(bf16[288,256]{1,0:T(8,128)(2,1)S(1)} %shard_map.81), channel_id=2, replica_groups=mesh['z'=16,'x'=4,'yl'=2,'yh'=2,'c'=2] {'yh','c'}, dimensions={0}, use_global_device_ids=true | all-gather | bytes 737280 | tf_op jit(solution)/shard_map/all_gather | solution.py:202
  120.3 0.8 shard_map.82
  (3 shorter events, 0.1 us)
Async XLA Ops:
  0.6 36.0 %copy-start = (bf16[128,256]{1,0:T(8,128)(2,1)S(1)}, bf16[128,256]{1,0:T(8,128)(2,1)}, u32[]{:S(2)}) copy-start(bf16[128,256]{1,0:T(8,128)(2,1)} %param.9) | copy-start | bytes 196612
  0.6 0.7 copy-start.4
  1.3 0.9 copy-start.1
  2.3 0.8 copy-start.3
  19.0 30.4 %all-to-all-start.1 = ((bf16[16,40,256]{2,1,0:T(8,128)(2,1)}), bf16[16,40,256]{2,1,0:T(8,128)(2,1)S(1)}, u32[]{:S(2)}, u32[]{:S(2)}) async-start(bf16[16,40,256]{2,1,0:T(8,128)(2,1)} %shard_map.77), calls=%async_computation.1 | async-start | bytes 655360 | tf_op jit(solution)/shard_map/all_to_all | solution.py:175
  35.8 13.5 %copy-start.2 = (bf16[256,256]{1,0:T(8,128)(2,1)S(1)}, bf16[256,256]{1,0:T(8,128)(2,1)}, u32[]{:S(2)}) copy-start(bf16[256,256]{1,0:T(8,128)(2,1)} %weight.1) | copy-start | bytes 393220
  36.6 6.7 %collective-permute-start = (bf16[64,256]{1,0:T(8,128)(2,1)S(1)}, bf16[64,256]{1,0:T(8,128)(2,1)S(1)}, u32[]{:S(2)}, u32[]{:S(2)}) collective-permute-start(bf16[64,256]{1,0:T(8,128)(2,1)S(1)} %pad_maximum_fusion), channel_id=1, source_target_pairs={{0,0},{1,4},{2,8},{3,12},{4,1},{5,5},{6,9},{7,13},{8,2},{9,6},{10,... | collective-permute-start | bytes 98312 | tf_op jit(solution)/shard_map/ppermute | solution.py:159
  93.3 15.5 %all-to-all-start.4 = ((bf16[8,144,256]{2,1,0:T(8,128)(2,1)}), bf16[8,144,256]{2,1,0:T(8,128)(2,1)S(1)}, u32[]{:S(2)}, u32[]{:S(2)}) async-start(bf16[8,144,256]{2,1,0:T(8,128)(2,1)} %shard_map.80), calls=%async_computation.4 | async-start | bytes 1179648 | tf_op jit(solution)/shard_map/all_to_all | solution.py:200
  96.8 12.0 %collective-permute-start.1 = (bf16[32,256]{1,0:T(8,128)(2,1)S(1)}, bf16[32,256]{1,0:T(8,128)(2,1)S(1)}, u32[]{:S(2)}, u32[]{:S(2)}) collective-permute-start(bf16[32,256]{1,0:T(8,128)(2,1)S(1)} %get-tuple-element.10), channel_id=1, source_target_pairs={{0,0},{1,4},{2,8},{3,12},{4,1},{5,5},{6,9},{7,13},{8,2},{9,6},{10,... | collective-permute-start | bytes 49160 | tf_op jit(solution)/shard_map/ppermute | solution.py:188

commit v4 on v3

--- a/solution.py
+++ b/solution.py
@@ -11,6 +11,9 @@
 Z, K8, R4, PL = 16, 8, 4, 32
 Q, W = 32, 256
 PARAMS = pltpu.CompilerParams(vmem_limit_bytes=24 * 1024 * 1024)
+
+
+FULL = 62 * 1024 * 1024
 
 
 def where_am_i():
@@ -38,10 +41,12 @@
     )(*args)
 
 
-def words_body(place, bits_far, features_far, out, bits, features, sems):
+def words_body(place_far, bits_far, features_far, grads_far, out, place, bits, features, grads, sems):
     fetches = [
-        pltpu.make_async_copy(bits_far, bits, sems.at[0]),
-        pltpu.make_async_copy(features_far, features, sems.at[1]),
+        pltpu.make_async_copy(place_far, place, sems.at[0]),
+        pltpu.make_async_copy(bits_far, bits, sems.at[1]),
+        pltpu.make_async_copy(features_far, features, sems.at[2]),
+        pltpu.make_async_copy(grads_far, grads, sems.at[3]),
     ]
     for fetch in fetches:
         fetch.start()
@@ -50,16 +55,20 @@
     lane = lax.broadcasted_iota(I32, (32, 512), 1)
     spread = jnp.where(lane // 16 == lax.broadcasted_iota(I32, (32, 512), 0), 1.0, 0.0).astype(BF)
     column = lax.broadcasted_iota(I32, (8, 512), 1) % 16
+    fetches[0].wait()
     at = jnp.broadcast_to(place[...].astype(F32), (8, 32)).astype(BF)
     key = jnp.dot(at, spread, preferred_element_type=F32).astype(I32) * 16 + column
     hot = jnp.where(want == key[0:1, :], 1.0, 0.0).astype(BF)
-    for fetch in fetches:
-        fetch.wait()
+    fetches[1].wait()
     dense = jnp.dot(hot, bits[...].astype(F32).astype(BF), preferred_element_type=F32).astype(BF)
     for k in range(K8):
         out[k, 0:32, 0:128] = dense[k * 64 : k * 64 + 32]
         out[k, 0:32, 128:256] = dense[k * 64 + 32 : k * 64 + 64]
+    fetches[2].wait()
+    fetches[3].wait()
+    for k in range(K8):
         out[k, 32:160, :] = features[...]
+        out[k, 160:192, :] = grads[(k % 4) * 32 : (k % 4) * 32 + 32, :]
 
 
 def unpacked(words):
@@ -76,7 +85,7 @@
     return lax.dot_general(block, source, (((0,), (0,)), ((), ())), preferred_element_type=F32)
 
 
-def forward_body(plane, out):
+def forward_body(plane, out, own):
     block = jnp.concatenate([unpacked(plane[k, 0:32, :]) for k in range(K8)], axis=1)
     source = plane[:, 32:160, :].reshape(K8 * 128, W)
     part = jnp.dot(block, source, preferred_element_type=F32)
@@ -87,6 +96,9 @@
         lanes = degree[0:8, (z // 4) * 128 : (z // 4 + 1) * 128]
         tail = jnp.concatenate([lanes, jnp.zeros_like(lanes)], axis=1)
         out[z] = jnp.concatenate([part[z * 32 : (z + 1) * 32], tail], axis=0).astype(BF)
+    x1, q, r = where_am_i()
+    own[0:32, :] = plane[x1 * 4 + r, pl.ds(pl.multiple_of(32 + q * 32, 32), 32), :]
+    own[32:64, :] = plane[x1 * 4 + r, 160:192, :]
 
 
 def middle_body(parts, own, weight, act, back, pushed, term):
@@ -109,11 +121,6 @@
     term[...] = over_rows(hidden, upstream).astype(BF)
 
 
-def two_parts(value):
-    high = value.astype(BF).astype(F32)
-    return jnp.concatenate([high, value - high], axis=0).astype(BF)
-
-
 def send_body(terms, pushed, out):
     extra = jnp.sum(terms[...].astype(F32), axis=0)
     message = jnp.concatenate([pushed[...].astype(F32), extra], axis=0).astype(BF)
@@ -125,53 +132,53 @@
     x1, q, r = where_am_i()
     received = gathered[...].astype(F32)
     source = received[:, 0:32].reshape(Z * Q, W).astype(BF)
-    extra = two_parts(jnp.sum(received[:, 32:40], axis=0))
+    extra = jnp.sum(received[:, 32:40], axis=0)
     for k in range(K8):
         total[k] = over_rows(unpacked(plane[k, 0:32, :]), source)
     rows = pl.ds(pl.multiple_of(q * 32, 32), 32)
     total[x1 * 4 + r, rows, :] = total[x1 * 4 + r, rows, :] + hidden_grad[...]
     for k in range(K8):
-        out[k, 0:128, :] = total[k].astype(BF)
-        out[k, 128:144, :] = extra
+        out[k] = jnp.concatenate([total[k], extra], axis=0).astype(BF)
 
 
 def share_body(parts, act, out):
-    out[0:128, :] = jnp.sum(parts[:, 0:128, :].astype(F32), axis=0).astype(BF)
-    for k in range(K8):
-        out[128 + k * 16 : 144 + k * 16, :] = parts[k, 128:144, :]
-    out[256:288, :] = act[...]
+    values = parts[...].astype(F32)
+    out[0:128, :] = jnp.sum(values[:, 0:128], axis=0).astype(BF)
+    out[128:192, :] = values[:, 128:136].reshape(64, W).astype(BF)
+    out[192:224, :] = act[...]
 
 
 def finish_body(shares, activation, weight_grad, input_grad):
     input_grad[...] = jnp.sum(shares[:, 0:128, :].astype(F32), axis=0).astype(BF)
     for r in range(R4):
-        activation[r * 32 : (r + 1) * 32, :] = shares[r, 256:288, :]
+        activation[r * 32 : (r + 1) * 32, :] = shares[r, 192:224, :]
+        slices = shares[r, 128:192, :].astype(F32)
         for k in range(K8):
-            both = shares[r, 128 + k * 16 : 144 + k * 16, :].astype(F32)
-            weight_grad[k * 32 + r * 8 : k * 32 + r * 8 + 8, :] = both[0:8] + both[8:16]
+            weight_grad[k * 32 + r * 8 : k * 32 + r * 8 + 8, :] = slices[k * 8 : k * 8 + 8]
 
 
 def per_device(features, weight, out_grad, tile_place, tile_bits, back_place, back_bits):
-    x1, q, r = where_am_i()
-    quarter = jnp.concatenate(
-        [lax.dynamic_slice_in_dim(a, r * Q, Q, 0) for a in (features, out_grad)], axis=0
-    )
-    own = lax.ppermute(quarter, PLANE, swap_pairs())
-    near, far = pl.BlockSpec(memory_space=pltpu.VMEM), pl.BlockSpec(memory_space=pl.ANY)
+    near, far = pl.BlockSpec(memory_space=pltpu.VMEM), pl.BlockSpec(memory_space=pltpu.HBM)
     plane = pl.pallas_call(
         words_body,
-        out_shape=jax.ShapeDtypeStruct((K8, 160, W), BF),
-        in_specs=[near, far, far],
+        out_shape=jax.ShapeDtypeStruct((K8, 192, W), BF),
+        in_specs=[far] * 4,
         out_specs=near,
         scratch_shapes=[
+            pltpu.VMEM((1, 32), I32),
             pltpu.VMEM((512, 128), I32),
             pltpu.VMEM((128, W), BF),
-            pltpu.SemaphoreType.DMA((2,)),
+            pltpu.VMEM((128, W), BF),
+            pltpu.SemaphoreType.DMA((4,)),
         ],
-        compiler_params=PARAMS,
-    )(back_place.reshape(1, 32), back_bits.reshape(512, 128), features)
+        compiler_params=pltpu.CompilerParams(vmem_limit_bytes=FULL),
+    )(back_place.reshape(1, 32), back_bits.reshape(512, 128), features, out_grad)
     plane = lax.all_to_all(plane, ROWS2, 0, 0)
-    parts = call(forward_body, jax.ShapeDtypeStruct((Z, 40, W), BF), plane)
+    parts, own = call(
+        forward_body,
+        (jax.ShapeDtypeStruct((Z, 40, W), BF), jax.ShapeDtypeStruct((2 * Q, W), BF)),
+        plane,
+    )
     parts = lax.all_to_all(parts, "z", 0, 0)
     act, hidden_grad, pushed, term = call(
         middle_body,
@@ -191,14 +198,14 @@
     gathered = lax.all_to_all(sent, "z", 0, 0)
     parts = pl.pallas_call(
         backward_body,
-        out_shape=jax.ShapeDtypeStruct((K8, 144, W), BF),
+        out_shape=jax.ShapeDtypeStruct((K8, 136, W), BF),
         in_specs=[near] * 3,
         out_specs=near,
         scratch_shapes=[pltpu.VMEM((K8, 128, W), F32)],
         compiler_params=PARAMS,
     )(plane, gathered, hidden_grad)
     parts = lax.all_to_all(parts, ROWS2, 0, 0)
-    share = call(share_body, jax.ShapeDtypeStruct((288, W), BF), parts, act)
+    share = call(share_body, jax.ShapeDtypeStruct((224, W), BF), parts, act)
     shares = lax.all_gather(share, REP, axis=0)
     return call(
         finish_body,

time: 122 us -> 120 us (0.984)
  blocking collectives: 67 us -> 98 us
  starting transfers between devices: 35.7 us -> 13.8 us
  waiting for transfers between devices: 9.34 us -> 1.71 us
  local copies, waits for them, and re-layouts: 3.24 us -> 0.01 us
    all_to_all x0 -> x1, blocking collectives: none -> 31.3 us  [per_device(): parts = lax.all_to_all(parts, 'z', 0, 0)]
    all_to_all x1 -> x0, starting transfers between devices: 16.8 us -> none  [per_device(): parts = lax.all_to_all(parts, 'z', 0, 0)]
    all_to_all x1 -> x0, waiting for transfers between devices: 6.05 us -> none  [per_device(): parts = lax.all_to_all(parts, 'z', 0, 0)]
    ppermute x1 -> x0, starting transfers between devices: 5.08 us -> none  [per_device(): own = lax.ppermute(quarter, PLANE, swap_pairs())]
    unnamed x10 -> x2, local copies, waits for them, and re-layouts: 2.48 us -> 0.01 us
    pallas_call x2, Pallas kernels: 2.25 us -> 3.87 us  [the longest x1 2.24 us: per_device(): pl.pallas_call(words_body, out_shape=jax.ShapeDtypeStruct((K8, 192, W), B...]
    ppermute x1 -> x0, waiting for transfers between devices: 1.58 us -> none  [per_device(): own = lax.ppermute(quarter, PLANE, swap_pairs())]
  transfers between devices with their start and end apart: 4 -> 2, of which waited for: 3 -> 1; matrix products, arithmetic and copies ran while one was open for 1% -> 0% of each run, Pallas kernels for 0% -> 0%
where the time goes in v4:
time: 120 us
  blocking collectives  98 us (82%)
  starting transfers between devices  13.8 us (12%)
  Pallas kernels  5.9 us (5%)
  waiting for transfers between devices  1.71 us (1%)
    all_to_all x1, blocking collectives, per_device(): parts = lax.all_to_all(parts, 'z', 0, 0)  31.3 us
    all_to_all x1, blocking collectives, per_device(): terms = lax.all_to_all(term.reshape(PL, 8, W), PLANE, 0, 0)  20.7 us
    all_to_all x1, blocking collectives, per_device(): gathered = lax.all_to_all(sent, 'z', 0, 0)  20.6 us
    all_to_all x1, blocking collectives, per_device(): plane = lax.all_to_all(plane, ROWS2, 0, 0)  14.6 us
    all_gather x1, blocking collectives, per_device(): shares = lax.all_gather(share, REP, axis=0)  10.8 us
    ppermute x1, starting transfers between devices, per_device(): act = lax.ppermute(act, PLANE, swap_pairs())  10.2 us
    all_to_all x1, starting transfers between devices, per_device(): parts = lax.all_to_all(parts, ROWS2, 0, 0)  3.54 us
  transfers between devices with their start and end apart: 2, of which 1 were waited for; matrix products, arithmetic and copies ran while one was open for 0% of the time, Pallas kernels for 0%

profile of v4, /device:TPU:1, one launch (start us, length us, event | category | flops | bytes accessed | tf_op | source)
XLA Modules:
  0.0 120.1 jit_solution(5791065491346462931)
XLA Ops:
  0.6 2.2 %shard_map.76 = bf16[8,192,256]{2,1,0:T(8,128)(2,1)} custom-call(s32[1,32]{1,0:T(1,128)} %bitcast.7, s32[512,128]{1,0:T(8,128)} %bitcast.6, bf16[128,256]{1,0:T(8,128)(2,1)} %features_far.1, bf16[128,256]{1,0:T(8,128)(2,1)} %grads_far.1), custom_call_target="tpu_custom_call" | custom-call | tf_op jit(solution)/shard_map/pallas_call | solution.py:162
  2.9 14.6 %all_to_all.25.plane = bf16[8,192,256]{2,1,0:T(8,128)(2,1)S(1)} all-to-all(bf16[8,192,256]{2,1,0:T(8,128)(2,1)} %shard_map.76), channel_id=1, replica_groups=mesh['z'=16,'x'=4,'yl'=2,'yh'=2,'c'=2] {'x','yl'}, dimensions={0} | all-to-all | bytes 1572864 | tf_op jit(solution)/shard_map/all_to_all | solution.py:176
  17.4 0.7 shard_map.77
  18.2 0.0 copy-start
  18.2 31.3 %all_to_all.26.parts = bf16[16,40,256]{2,1,0:T(8,128)(2,1)S(1)} all-to-all(bf16[16,40,256]{2,1,0:T(8,128)(2,1)S(1)} %get-tuple-element.9), channel_id=1, replica_groups=mesh['z'=16,'x'=4,'yl'=2,'yh'=2,'c'=2] {'z'}, dimensions={0} | all-to-all | bytes 655360 | tf_op jit(solution)/shard_map/all_to_all | solution.py:182
  49.5 0.0 copy-done
  49.5 0.4 shard_map.78
  49.9 20.7 %all_to_all.27.terms = bf16[32,8,256]{2,1,0:T(8,128)(2,1)S(1)} all-to-all(bf16[32,8,256]{2,1,0:T(8,128)(2,1)S(1)} %bitcast.5), channel_id=1, replica_groups=mesh['z'=16,'x'=4,'yl'=2,'yh'=2,'c'=2] {'x','yl','yh','c'}, dimensions={0} | all-to-all | bytes 262144 | tf_op jit(solution)/shard_map/all_to_all | solution.py:196
  70.6 20.6 %all_to_all.28.gathered = bf16[16,40,256]{2,1,0:T(8,128)(2,1)S(1)} all-to-all(bf16[16,40,256]{2,1,0:T(8,128)(2,1)S(1)} %shard_map.79), channel_id=1, replica_groups=mesh['z'=16,'x'=4,'yl'=2,'yh'=2,'c'=2] {'z'}, dimensions={0} | all-to-all | bytes 655360 | tf_op jit(solution)/shard_map/all_to_all | solution.py:198
  91.3 1.6 %shard_map.80 = bf16[8,136,256]{2,1,0:T(8,128)(2,1)} custom-call(bf16[8,192,256]{2,1,0:T(8,128)(2,1)S(1)} %all_to_all.25.plane, bf16[16,40,256]{2,1,0:T(8,128)(2,1)S(1)} %all_to_all.28.gathered, f32[32,256]{1,0:T(8,128)S(1)} %get-tuple-element.13.hidden_grad), custom_call_target="tpu_custom_call" | custom-call | tf_op jit(solution)/shard_map/pallas_call | solution.py:199
  92.9 3.5 %all-to-all-start.4 = ((bf16[8,136,256]{2,1,0:T(8,128)(2,1)}), bf16[8,136,256]{2,1,0:T(8,128)(2,1)S(1)}, u32[]{:S(2)}, u32[]{:S(2)}) async-start(bf16[8,136,256]{2,1,0:T(8,128)(2,1)} %shard_map.80), calls=%async_computation.4 | async-start | bytes 1114112 | tf_op jit(solution)/shard_map/all_to_all | solution.py:207
  96.4 10.2 %collective-permute-start = (bf16[32,256]{1,0:T(8,128)(2,1)S(1)}, bf16[32,256]{1,0:T(8,128)(2,1)S(1)}, u32[]{:S(2)}, u32[]{:S(2)}) collective-permute-start(bf16[32,256]{1,0:T(8,128)(2,1)S(1)} %get-tuple-element.14), channel_id=1, source_target_pairs={{0,0},{1,4},{2,8},{3,12},{4,1},{5,5},{6,9},{7,13},{8,2},{9,6},{10,... | collective-permute-start | bytes 49160 | tf_op jit(solution)/shard_map/ppermute | solution.py:195
  106.7 1.7 %collective-permute-done.act = bf16[32,256]{1,0:T(8,128)(2,1)S(1)} collective-permute-done((bf16[32,256]{1,0:T(8,128)(2,1)S(1)}, bf16[32,256]{1,0:T(8,128)(2,1)S(1)}, u32[]{:S(2)}, u32[]{:S(2)}) %collective-permute-start) | collective-permute-done | bytes 16416 | tf_op jit(solution)/shard_map/ppermute | solution.py:195
  108.4 0.0 all-to-all-done.4.parts
  108.4 0.1 shard_map.81
  108.5 10.8 %all-gather = bf16[896,256]{1,0:T(8,128)(2,1)S(1)} all-gather(bf16[224,256]{1,0:T(8,128)(2,1)S(1)} %shard_map.81), channel_id=2, replica_groups=mesh['z'=16,'x'=4,'yl'=2,'yh'=2,'c'=2] {'yh','c'}, dimensions={0}, use_global_device_ids=true | all-gather | bytes 573440 | tf_op jit(solution)/shard_map/all_gather | solution.py:209
  119.3 0.8 shard_map.82
  (1 shorter events, 0.0 us)
Async XLA Ops:
  18.2 31.3 %copy-start = (bf16[256,256]{1,0:T(8,128)(2,1)S(1)}, bf16[256,256]{1,0:T(8,128)(2,1)}, u32[]{:S(2)}) copy-start(bf16[256,256]{1,0:T(8,128)(2,1)} %weight.1) | copy-start | bytes 393220
  92.9 15.5 %all-to-all-start.4 = ((bf16[8,136,256]{2,1,0:T(8,128)(2,1)}), bf16[8,136,256]{2,1,0:T(8,128)(2,1)S(1)}, u32[]{:S(2)}, u32[]{:S(2)}) async-start(bf16[8,136,256]{2,1,0:T(8,128)(2,1)} %shard_map.80), calls=%async_computation.4 | async-start | bytes 1114112 | tf_op jit(solution)/shard_map/all_to_all | solution.py:207
  96.4 12.0 %collective-permute-start = (bf16[32,256]{1,0:T(8,128)(2,1)S(1)}, bf16[32,256]{1,0:T(8,128)(2,1)S(1)}, u32[]{:S(2)}, u32[]{:S(2)}) collective-permute-start(bf16[32,256]{1,0:T(8,128)(2,1)S(1)} %get-tuple-element.14), channel_id=1, source_target_pairs={{0,0},{1,4},{2,8},{3,12},{4,1},{5,5},{6,9},{7,13},{8,2},{9,6},{10,... | collective-permute-start | bytes 49160 | tf_op jit(solution)/shard_map/ppermute | solution.py:195

commit v5 on v4

--- a/solution.py
+++ b/solution.py
@@ -44,13 +44,13 @@
 def words_body(place_far, bits_far, features_far, grads_far, out, place, bits, features, grads, sems):
     fetches = [
         pltpu.make_async_copy(place_far, place, sems.at[0]),
-        pltpu.make_async_copy(bits_far, bits, sems.at[1]),
-        pltpu.make_async_copy(features_far, features, sems.at[2]),
-        pltpu.make_async_copy(grads_far, grads, sems.at[3]),
+        pltpu.make_async_copy(features_far, features, sems.at[1]),
+        pltpu.make_async_copy(grads_far, grads, sems.at[2]),
+        pltpu.make_async_copy(bits_far, bits, sems.at[3]),
     ]
     for fetch in fetches:
         fetch.start()
-    row = lax.broadcasted_iota(I32, (512, 512), 0)
+    row = lax.broadcasted_iota(I32, (512, 128), 0)
     want = (((row // 4) % 16) * 2 + row // 256) * 16 + ((row // 64) % 4) * 4 + row % 4
     lane = lax.broadcasted_iota(I32, (32, 512), 1)
     spread = jnp.where(lane // 16 == lax.broadcasted_iota(I32, (32, 512), 0), 1.0, 0.0).astype(BF)
@@ -58,17 +58,19 @@
     fetches[0].wait()
     at = jnp.broadcast_to(place[...].astype(F32), (8, 32)).astype(BF)
     key = jnp.dot(at, spread, preferred_element_type=F32).astype(I32) * 16 + column
-    hot = jnp.where(want == key[0:1, :], 1.0, 0.0).astype(BF)
+    hot = jnp.concatenate(
+        [jnp.where(want == key[0:1, c * 128 : (c + 1) * 128], 1.0, 0.0) for c in range(4)], axis=1
+    ).astype(BF)
     fetches[1].wait()
+    fetches[2].wait()
+    for k in range(K8):
+        out[k, 32:160, :] = features[...]
+        out[k, 160:192, :] = grads[(k % 4) * 32 : (k % 4) * 32 + 32, :]
+    fetches[3].wait()
     dense = jnp.dot(hot, bits[...].astype(F32).astype(BF), preferred_element_type=F32).astype(BF)
     for k in range(K8):
         out[k, 0:32, 0:128] = dense[k * 64 : k * 64 + 32]
         out[k, 0:32, 128:256] = dense[k * 64 + 32 : k * 64 + 64]
-    fetches[2].wait()
-    fetches[3].wait()
-    for k in range(K8):
-        out[k, 32:160, :] = features[...]
-        out[k, 160:192, :] = grads[(k % 4) * 32 : (k % 4) * 32 + 32, :]
 
 
 def unpacked(words):
@@ -93,9 +95,9 @@
     ones = jnp.where(fourth == lax.broadcasted_iota(I32, (16, 1024), 0), 1.0, 0.0).astype(BF)
     degree = lax.dot_general(ones, block, (((1,), (1,)), ((), ())), preferred_element_type=F32)
     for z in range(Z):
+        mine = part[z * 32 : (z + 1) * 32]
         lanes = degree[0:8, (z // 4) * 128 : (z // 4 + 1) * 128]
-        tail = jnp.concatenate([lanes, jnp.zeros_like(lanes)], axis=1)
-        out[z] = jnp.concatenate([part[z * 32 : (z + 1) * 32], tail], axis=0).astype(BF)
+        out[z] = jnp.concatenate([mine[:, 0:128], mine[:, 128:256], lanes], axis=0).astype(BF)
     x1, q, r = where_am_i()
     own[0:32, :] = plane[x1 * 4 + r, pl.ds(pl.multiple_of(32 + q * 32, 32), 32), :]
     own[32:64, :] = plane[x1 * 4 + r, 160:192, :]
@@ -103,12 +105,13 @@
 
 def middle_body(parts, own, weight, act, back, pushed, term):
     total = jnp.sum(parts[...].astype(F32), axis=0)
-    degree = jnp.sum(total[32:36, 0:128], axis=0, keepdims=True)
+    degree = jnp.sum(total[64:68], axis=0, keepdims=True)
     first = (lax.axis_index("z") % 4) * 32
     pick = lax.broadcasted_iota(I32, (32, 128), 1) == lax.broadcasted_iota(I32, (32, 128), 0) + first
     counted = jnp.sum(jnp.where(pick, degree, 0.0), axis=1, keepdims=True)
     scaling = lax.rsqrt(1.0 + counted)
-    hidden = (own[0:32, :].astype(F32) + total[0:32] * scaling).astype(BF)
+    gathered = jnp.concatenate([total[0:32], total[32:64]], axis=1)
+    hidden = (own[0:32, :].astype(F32) + gathered * scaling).astype(BF)
     logits = jnp.dot(hidden, weight[...], preferred_element_type=F32)
     gate = jax.nn.sigmoid(logits)
     act[...] = (logits * gate).astype(BF)
@@ -128,17 +131,17 @@
         out[z] = message
 
 
-def backward_body(plane, gathered, hidden_grad, out, total):
+def backward_body(plane, gathered, hidden_grad, out):
     x1, q, r = where_am_i()
-    received = gathered[...].astype(F32)
-    source = received[:, 0:32].reshape(Z * Q, W).astype(BF)
-    extra = jnp.sum(received[:, 32:40], axis=0)
+    received = gathered[...]
+    source = received[:, 0:32].reshape(Z * Q, W)
+    extra = jnp.sum(received[:, 32:40].astype(F32), axis=0)
+    own = hidden_grad[...]
+    placed = jnp.concatenate([jnp.where(q == t, own, 0.0) for t in range(4)], axis=0)
     for k in range(K8):
-        total[k] = over_rows(unpacked(plane[k, 0:32, :]), source)
-    rows = pl.ds(pl.multiple_of(q * 32, 32), 32)
-    total[x1 * 4 + r, rows, :] = total[x1 * 4 + r, rows, :] + hidden_grad[...]
-    for k in range(K8):
-        out[k] = jnp.concatenate([total[k], extra], axis=0).astype(BF)
+        part = over_rows(unpacked(plane[k, 0:32, :]), source)
+        part = part + jnp.where(x1 * 4 + r == k, placed, 0.0)
+        out[k] = jnp.concatenate([part, extra], axis=0).astype(BF)
 
 
 def share_body(parts, act, out):
@@ -176,7 +179,7 @@
     plane = lax.all_to_all(plane, ROWS2, 0, 0)
     parts, own = call(
         forward_body,
-        (jax.ShapeDtypeStruct((Z, 40, W), BF), jax.ShapeDtypeStruct((2 * Q, W), BF)),
+        (jax.ShapeDtypeStruct((Z, 72, 128), BF), jax.ShapeDtypeStruct((2 * Q, W), BF)),
         plane,
     )
     parts = lax.all_to_all(parts, "z", 0, 0)
@@ -196,14 +199,9 @@
     terms = lax.all_to_all(term.reshape(PL, 8, W), PLANE, 0, 0)
     sent = call(send_body, jax.ShapeDtypeStruct((Z, 40, W), BF), terms, pushed)
     gathered = lax.all_to_all(sent, "z", 0, 0)
-    parts = pl.pallas_call(
-        backward_body,
-        out_shape=jax.ShapeDtypeStruct((K8, 136, W), BF),
-        in_specs=[near] * 3,
-        out_specs=near,
-        scratch_shapes=[pltpu.VMEM((K8, 128, W), F32)],
-        compiler_params=PARAMS,
-    )(plane, gathered, hidden_grad)
+    parts = call(
+        backward_body, jax.ShapeDtypeStruct((K8, 136, W), BF), plane, gathered, hidden_grad
+    )
     parts = lax.all_to_all(parts, ROWS2, 0, 0)
     share = call(share_body, jax.ShapeDtypeStruct((224, W), BF), parts, act)
     shares = lax.all_gather(share, REP, axis=0)

time: 120 us -> 119 us (level)
  blocking collectives: 98 us -> 96.6 us
    pallas_call x1 -> x0, Pallas kernels: 1.62 us -> none  [per_device(): pl.pallas_call(backward_body, out_shape=jax.ShapeDtypeStruct((K8, 136, W)...]
    pallas_call x5 -> x6, Pallas kernels: 2.03 us -> 3.64 us  [call(): pl.pallas_call(body, out_shape=shapes, in_specs=[pl.BlockSpec(memory_spac...]
where the time goes in v5:
time: 119 us
  blocking collectives  96.6 us (81%)
  starting transfers between devices  13.8 us (12%)
  Pallas kernels  5.91 us (5%)
  waiting for transfers between devices  1.71 us (1%)
    all_to_all x1, blocking collectives, per_device(): parts = lax.all_to_all(parts, 'z', 0, 0)  30.7 us
    all_to_all x1, blocking collectives, per_device(): gathered = lax.all_to_all(sent, 'z', 0, 0)  20.4 us
    all_to_all x1, blocking collectives, per_device(): terms = lax.all_to_all(term.reshape(PL, 8, W), PLANE, 0, 0)  20 us
    all_to_all x1, blocking collectives, per_device(): plane = lax.all_to_all(plane, ROWS2, 0, 0)  14.5 us
    all_gather x1, blocking collectives, per_device(): shares = lax.all_gather(share, REP, axis=0)  10.8 us
    ppermute x1, starting transfers between devices, per_device(): act = lax.ppermute(act, PLANE, swap_pairs())  10.2 us
    pallas_call x6, Pallas kernels, call(): pl.pallas_call(body, out_shape=shapes, in_specs=[pl.BlockSpec(memory_spac...  3.64 us
    all_to_all x1, starting transfers between devices, per_device(): parts = lax.all_to_all(parts, ROWS2, 0, 0)  3.54 us
  transfers between devices with their start and end apart: 2, of which 1 were waited for; matrix products, arithmetic and copies ran while one was open for 0% of the time, Pallas kernels for 0%

profile of v5, /device:TPU:1, one launch (start us, length us, event | category | flops | bytes accessed | tf_op | source)
XLA Modules:
  0.0 118.7 jit_solution(6894165107050180358)
XLA Ops:
  0.6 2.3 %shard_map.76 = bf16[8,192,256]{2,1,0:T(8,128)(2,1)} custom-call(s32[1,32]{1,0:T(1,128)} %bitcast.7, s32[512,128]{1,0:T(8,128)} %bitcast.6, bf16[128,256]{1,0:T(8,128)(2,1)} %features_far.1, bf16[128,256]{1,0:T(8,128)(2,1)} %grads_far.1), custom_call_target="tpu_custom_call" | custom-call | tf_op jit(solution)/shard_map/pallas_call | solution.py:165
  2.9 14.5 %all_to_all.25.plane = bf16[8,192,256]{2,1,0:T(8,128)(2,1)S(1)} all-to-all(bf16[8,192,256]{2,1,0:T(8,128)(2,1)} %shard_map.76), channel_id=1, replica_groups=mesh['z'=16,'x'=4,'yl'=2,'yh'=2,'c'=2] {'x','yl'}, dimensions={0} | all-to-all | bytes 1572864 | tf_op jit(solution)/shard_map/all_to_all | solution.py:179
  17.5 0.7 shard_map.77
  18.2 0.0 copy-start
  18.2 30.7 %all_to_all.26.parts = bf16[16,72,128]{2,1,0:T(8,128)(2,1)S(1)} all-to-all(bf16[16,72,128]{2,1,0:T(8,128)(2,1)S(1)} %get-tuple-element.9), channel_id=1, replica_groups=mesh['z'=16,'x'=4,'yl'=2,'yh'=2,'c'=2] {'z'}, dimensions={0} | all-to-all | bytes 589824 | tf_op jit(solution)/shard_map/all_to_all | solution.py:185
  49.0 0.0 copy-done
  49.0 0.4 shard_map.78
  49.4 20.0 %all_to_all.27.terms = bf16[32,8,256]{2,1,0:T(8,128)(2,1)S(1)} all-to-all(bf16[32,8,256]{2,1,0:T(8,128)(2,1)S(1)} %bitcast.5), channel_id=1, replica_groups=mesh['z'=16,'x'=4,'yl'=2,'yh'=2,'c'=2] {'x','yl','yh','c'}, dimensions={0} | all-to-all | bytes 262144 | tf_op jit(solution)/shard_map/all_to_all | solution.py:199
  69.5 20.4 %all_to_all.28.gathered = bf16[16,40,256]{2,1,0:T(8,128)(2,1)S(1)} all-to-all(bf16[16,40,256]{2,1,0:T(8,128)(2,1)S(1)} %shard_map.79), channel_id=1, replica_groups=mesh['z'=16,'x'=4,'yl'=2,'yh'=2,'c'=2] {'z'}, dimensions={0} | all-to-all | bytes 655360 | tf_op jit(solution)/shard_map/all_to_all | solution.py:201
  89.9 1.6 %shard_map.80 = bf16[8,136,256]{2,1,0:T(8,128)(2,1)} custom-call(bf16[8,192,256]{2,1,0:T(8,128)(2,1)S(1)} %all_to_all.25.plane, bf16[16,40,256]{2,1,0:T(8,128)(2,1)S(1)} %all_to_all.28.gathered, f32[32,256]{1,0:T(8,128)S(1)} %get-tuple-element.13.hidden_grad), custom_call_target="tpu_custom_call" | custom-call | tf_op jit(solution)/shard_map/pallas_call | solution.py:35
  91.5 3.5 %all-to-all-start.4 = ((bf16[8,136,256]{2,1,0:T(8,128)(2,1)}), bf16[8,136,256]{2,1,0:T(8,128)(2,1)S(1)}, u32[]{:S(2)}, u32[]{:S(2)}) async-start(bf16[8,136,256]{2,1,0:T(8,128)(2,1)} %shard_map.80), calls=%async_computation.4 | async-start | bytes 1114112 | tf_op jit(solution)/shard_map/all_to_all | solution.py:205
  95.1 10.2 %collective-permute-start = (bf16[32,256]{1,0:T(8,128)(2,1)S(1)}, bf16[32,256]{1,0:T(8,128)(2,1)S(1)}, u32[]{:S(2)}, u32[]{:S(2)}) collective-permute-start(bf16[32,256]{1,0:T(8,128)(2,1)S(1)} %get-tuple-element.14), channel_id=1, source_target_pairs={{0,0},{1,4},{2,8},{3,12},{4,1},{5,5},{6,9},{7,13},{8,2},{9,6},{10,... | collective-permute-start | bytes 49160 | tf_op jit(solution)/shard_map/ppermute | solution.py:198
  105.3 1.7 %collective-permute-done.act = bf16[32,256]{1,0:T(8,128)(2,1)S(1)} collective-permute-done((bf16[32,256]{1,0:T(8,128)(2,1)S(1)}, bf16[32,256]{1,0:T(8,128)(2,1)S(1)}, u32[]{:S(2)}, u32[]{:S(2)}) %collective-permute-start) | collective-permute-done | bytes 16416 | tf_op jit(solution)/shard_map/ppermute | solution.py:198
  107.0 0.0 all-to-all-done.4.parts
  107.0 0.1 shard_map.81
  107.1 10.8 %all-gather = bf16[896,256]{1,0:T(8,128)(2,1)S(1)} all-gather(bf16[224,256]{1,0:T(8,128)(2,1)S(1)} %shard_map.81), channel_id=2, replica_groups=mesh['z'=16,'x'=4,'yl'=2,'yh'=2,'c'=2] {'yh','c'}, dimensions={0}, use_global_device_ids=true | all-gather | bytes 573440 | tf_op jit(solution)/shard_map/all_gather | solution.py:207
  117.9 0.8 shard_map.82
  (1 shorter events, 0.0 us)
Async XLA Ops:
  18.2 30.8 %copy-start = (bf16[256,256]{1,0:T(8,128)(2,1)S(1)}, bf16[256,256]{1,0:T(8,128)(2,1)}, u32[]{:S(2)}) copy-start(bf16[256,256]{1,0:T(8,128)(2,1)} %weight.1) | copy-start | bytes 393220
  91.5 15.5 %all-to-all-start.4 = ((bf16[8,136,256]{2,1,0:T(8,128)(2,1)}), bf16[8,136,256]{2,1,0:T(8,128)(2,1)S(1)}, u32[]{:S(2)}, u32[]{:S(2)}) async-start(bf16[8,136,256]{2,1,0:T(8,128)(2,1)} %shard_map.80), calls=%async_computation.4 | async-start | bytes 1114112 | tf_op jit(solution)/shard_map/all_to_all | solution.py:205
  95.1 12.0 %collective-permute-start = (bf16[32,256]{1,0:T(8,128)(2,1)S(1)}, bf16[32,256]{1,0:T(8,128)(2,1)S(1)}, u32[]{:S(2)}, u32[]{:S(2)}) collective-permute-start(bf16[32,256]{1,0:T(8,128)(2,1)S(1)} %get-tuple-element.14), channel_id=1, source_target_pairs={{0,0},{1,4},{2,8},{3,12},{4,1},{5,5},{6,9},{7,13},{8,2},{9,6},{10,... | collective-permute-start | bytes 49160 | tf_op jit(solution)/shard_map/ppermute | solution.py:198

commit v6 on v5

--- a/solution.py
+++ b/solution.py
@@ -41,7 +41,7 @@
     )(*args)
 
 
-def words_body(place_far, bits_far, features_far, grads_far, out, place, bits, features, grads, sems):
+def words_body(place_far, bits_far, features_far, grads_far, out, place, bits, features, grads, words, sems):
     fetches = [
         pltpu.make_async_copy(place_far, place, sems.at[0]),
         pltpu.make_async_copy(features_far, features, sems.at[1]),
@@ -63,14 +63,23 @@
     ).astype(BF)
     fetches[1].wait()
     fetches[2].wait()
+    puts = []
     for k in range(K8):
-        out[k, 32:160, :] = features[...]
-        out[k, 160:192, :] = grads[(k % 4) * 32 : (k % 4) * 32 + 32, :]
+        quarter = grads.at[pl.ds((k % 4) * 32, 32), :]
+        puts.append(pltpu.make_async_copy(features, out.at[k, pl.ds(32, 128), :], sems.at[4 + k]))
+        puts.append(pltpu.make_async_copy(quarter, out.at[k, pl.ds(160, 32), :], sems.at[12 + k]))
+    for put in puts:
+        put.start()
     fetches[3].wait()
     dense = jnp.dot(hot, bits[...].astype(F32).astype(BF), preferred_element_type=F32).astype(BF)
     for k in range(K8):
-        out[k, 0:32, 0:128] = dense[k * 64 : k * 64 + 32]
-        out[k, 0:32, 128:256] = dense[k * 64 + 32 : k * 64 + 64]
+        words[k, :, 0:128] = dense[k * 64 : k * 64 + 32]
+        words[k, :, 128:256] = dense[k * 64 + 32 : k * 64 + 64]
+    last = pltpu.make_async_copy(words, out.at[:, pl.ds(0, 32), :], sems.at[20])
+    last.start()
+    for put in puts:
+        put.wait()
+    last.wait()
 
 
 def unpacked(words):
@@ -87,7 +96,7 @@
     return lax.dot_general(block, source, (((0,), (0,)), ((), ())), preferred_element_type=F32)
 
 
-def forward_body(plane, out, own):
+def forward_body(plane, out, own, turned):
     block = jnp.concatenate([unpacked(plane[k, 0:32, :]) for k in range(K8)], axis=1)
     source = plane[:, 32:160, :].reshape(K8 * 128, W)
     part = jnp.dot(block, source, preferred_element_type=F32)
@@ -101,6 +110,7 @@
     x1, q, r = where_am_i()
     own[0:32, :] = plane[x1 * 4 + r, pl.ds(pl.multiple_of(32 + q * 32, 32), 32), :]
     own[32:64, :] = plane[x1 * 4 + r, 160:192, :]
+    turned[...] = block.T
 
 
 def middle_body(parts, own, weight, act, back, pushed, term):
@@ -131,7 +141,7 @@
         out[z] = message
 
 
-def backward_body(plane, gathered, hidden_grad, out):
+def backward_body(turned, gathered, hidden_grad, out):
     x1, q, r = where_am_i()
     received = gathered[...]
     source = received[:, 0:32].reshape(Z * Q, W)
@@ -139,7 +149,7 @@
     own = hidden_grad[...]
     placed = jnp.concatenate([jnp.where(q == t, own, 0.0) for t in range(4)], axis=0)
     for k in range(K8):
-        part = over_rows(unpacked(plane[k, 0:32, :]), source)
+        part = jnp.dot(turned[k * 128 : (k + 1) * 128, :], source, preferred_element_type=F32)
         part = part + jnp.where(x1 * 4 + r == k, placed, 0.0)
         out[k] = jnp.concatenate([part, extra], axis=0).astype(BF)
 
@@ -166,20 +176,25 @@
         words_body,
         out_shape=jax.ShapeDtypeStruct((K8, 192, W), BF),
         in_specs=[far] * 4,
-        out_specs=near,
+        out_specs=far,
         scratch_shapes=[
             pltpu.VMEM((1, 32), I32),
             pltpu.VMEM((512, 128), I32),
             pltpu.VMEM((128, W), BF),
             pltpu.VMEM((128, W), BF),
-            pltpu.SemaphoreType.DMA((4,)),
+            pltpu.VMEM((K8, 32, W), BF),
+            pltpu.SemaphoreType.DMA((21,)),
         ],
         compiler_params=pltpu.CompilerParams(vmem_limit_bytes=FULL),
     )(back_place.reshape(1, 32), back_bits.reshape(512, 128), features, out_grad)
     plane = lax.all_to_all(plane, ROWS2, 0, 0)
-    parts, own = call(
+    parts, own, turned = call(
         forward_body,
-        (jax.ShapeDtypeStruct((Z, 72, 128), BF), jax.ShapeDtypeStruct((2 * Q, W), BF)),
+        (
+            jax.ShapeDtypeStruct((Z, 72, 128), BF),
+            jax.ShapeDtypeStruct((2 * Q, W), BF),
+            jax.ShapeDtypeStruct((K8 * 128, Z * Q), BF),
+        ),
         plane,
     )
     parts = lax.all_to_all(parts, "z", 0, 0)
@@ -200,7 +215,7 @@
     sent = call(send_body, jax.ShapeDtypeStruct((Z, 40, W), BF), terms, pushed)
     gathered = lax.all_to_all(sent, "z", 0, 0)
     parts = call(
-        backward_body, jax.ShapeDtypeStruct((K8, 136, W), BF), plane, gathered, hidden_grad
+        backward_body, jax.ShapeDtypeStruct((K8, 136, W), BF), turned, gathered, hidden_grad
     )
     parts = lax.all_to_all(parts, ROWS2, 0, 0)
     share = call(share_body, jax.ShapeDtypeStruct((224, W), BF), parts, act)

time: 119 us -> 119 us (level)
  no operation moved by 1% of the time
where the time goes in v6:
time: 119 us; the launch traced here: 118 us
  blocking collectives  96.6 us (81%)
  starting transfers between devices  13.8 us (12%)
  Pallas kernels  5.48 us (5%)
  waiting for transfers between devices  1.71 us (1%)
    all_to_all x1, blocking collectives, per_device(): parts = lax.all_to_all(parts, 'z', 0, 0)  30.7 us
    all_to_all x1, blocking collectives, per_device(): gathered = lax.all_to_all(sent, 'z', 0, 0)  20.4 us
    all_to_all x1, blocking collectives, per_device(): terms = lax.all_to_all(term.reshape(PL, 8, W), PLANE, 0, 0)  20 us
    all_to_all x1, blocking collectives, per_device(): plane = lax.all_to_all(plane, ROWS2, 0, 0)  14.5 us
    all_gather x1, blocking collectives, per_device(): shares = lax.all_gather(share, REP, axis=0)  10.8 us
    ppermute x1, starting transfers between devices, per_device(): act = lax.ppermute(act, PLANE, swap_pairs())  10.2 us
    all_to_all x1, starting transfers between devices, per_device(): parts = lax.all_to_all(parts, ROWS2, 0, 0)  3.54 us
    pallas_call x6, Pallas kernels, call(): pl.pallas_call(body, out_shape=shapes, in_specs=[pl.BlockSpec(memory_spac...  3.28 us
  transfers between devices with their start and end apart: 2, of which 1 were waited for; matrix products, arithmetic and copies ran while one was open for 0% of the time, Pallas kernels for 0%

profile of v6, /device:TPU:1, one launch (start us, length us, event | category | flops | bytes accessed | tf_op | source)
XLA Modules:
  0.0 118.3 jit_solution(16970275436866287465)
XLA Ops:
  0.6 2.2 %shard_map.76 = bf16[8,192,256]{2,1,0:T(8,128)(2,1)} custom-call(s32[1,32]{1,0:T(1,128)} %bitcast.7, s32[512,128]{1,0:T(8,128)} %bitcast.6, bf16[128,256]{1,0:T(8,128)(2,1)} %features_far.1, bf16[128,256]{1,0:T(8,128)(2,1)} %grads_far.1), custom_call_target="tpu_custom_call" | custom-call | tf_op jit(solution)/shard_map/pallas_call | solution.py:175
  2.8 14.5 %all_to_all.25.plane = bf16[8,192,256]{2,1,0:T(8,128)(2,1)S(1)} all-to-all(bf16[8,192,256]{2,1,0:T(8,128)(2,1)} %shard_map.76), channel_id=1, replica_groups=mesh['z'=16,'x'=4,'yl'=2,'yh'=2,'c'=2] {'x','yl'}, dimensions={0} | all-to-all | bytes 1572864 | tf_op jit(solution)/shard_map/all_to_all | solution.py:190
  17.4 0.7 shard_map.77
  18.1 0.0 copy-start
  18.1 30.7 %all_to_all.26.parts = bf16[16,72,128]{2,1,0:T(8,128)(2,1)S(1)} all-to-all(bf16[16,72,128]{2,1,0:T(8,128)(2,1)S(1)} %get-tuple-element.11), channel_id=1, replica_groups=mesh['z'=16,'x'=4,'yl'=2,'yh'=2,'c'=2] {'z'}, dimensions={0} | all-to-all | bytes 589824 | tf_op jit(solution)/shard_map/all_to_all | solution.py:200
  48.9 0.0 copy-done
  48.9 0.4 shard_map.78
  49.3 20.0 %all_to_all.27.terms = bf16[32,8,256]{2,1,0:T(8,128)(2,1)S(1)} all-to-all(bf16[32,8,256]{2,1,0:T(8,128)(2,1)S(1)} %bitcast.5), channel_id=1, replica_groups=mesh['z'=16,'x'=4,'yl'=2,'yh'=2,'c'=2] {'x','yl','yh','c'}, dimensions={0} | all-to-all | bytes 262144 | tf_op jit(solution)/shard_map/all_to_all | solution.py:214
  69.4 20.4 %all_to_all.28.gathered = bf16[16,40,256]{2,1,0:T(8,128)(2,1)S(1)} all-to-all(bf16[16,40,256]{2,1,0:T(8,128)(2,1)S(1)} %shard_map.79), channel_id=1, replica_groups=mesh['z'=16,'x'=4,'yl'=2,'yh'=2,'c'=2] {'z'}, dimensions={0} | all-to-all | bytes 655360 | tf_op jit(solution)/shard_map/all_to_all | solution.py:216
  89.8 1.3 %shard_map.80 = bf16[8,136,256]{2,1,0:T(8,128)(2,1)} custom-call(bf16[1024,512]{1,0:T(8,128)(2,1)S(1)} %get-tuple-element.10.turned, bf16[16,40,256]{2,1,0:T(8,128)(2,1)S(1)} %all_to_all.28.gathered, f32[32,256]{1,0:T(8,128)S(1)} %get-tuple-element.15.hidden_grad), custom_call_target="tpu_custom_call" | custom-call | tf_op jit(solution)/shard_map/pallas_call | solution.py:35
  91.1 3.5 %all-to-all-start.4 = ((bf16[8,136,256]{2,1,0:T(8,128)(2,1)}), bf16[8,136,256]{2,1,0:T(8,128)(2,1)S(1)}, u32[]{:S(2)}, u32[]{:S(2)}) async-start(bf16[8,136,256]{2,1,0:T(8,128)(2,1)} %shard_map.80), calls=%async_computation.4 | async-start | bytes 1114112 | tf_op jit(solution)/shard_map/all_to_all | solution.py:220
  94.6 10.2 %collective-permute-start = (bf16[32,256]{1,0:T(8,128)(2,1)S(1)}, bf16[32,256]{1,0:T(8,128)(2,1)S(1)}, u32[]{:S(2)}, u32[]{:S(2)}) collective-permute-start(bf16[32,256]{1,0:T(8,128)(2,1)S(1)} %get-tuple-element.16), channel_id=1, source_target_pairs={{0,0},{1,4},{2,8},{3,12},{4,1},{5,5},{6,9},{7,13},{8,2},{9,6},{10,... | collective-permute-start | bytes 49160 | tf_op jit(solution)/shard_map/ppermute | solution.py:213
  104.9 1.7 %collective-permute-done.act = bf16[32,256]{1,0:T(8,128)(2,1)S(1)} collective-permute-done((bf16[32,256]{1,0:T(8,128)(2,1)S(1)}, bf16[32,256]{1,0:T(8,128)(2,1)S(1)}, u32[]{:S(2)}, u32[]{:S(2)}) %collective-permute-start) | collective-permute-done | bytes 16416 | tf_op jit(solution)/shard_map/ppermute | solution.py:213
  106.6 0.0 all-to-all-done.4.parts
  106.6 0.1 shard_map.81
  106.7 10.8 %all-gather = bf16[896,256]{1,0:T(8,128)(2,1)S(1)} all-gather(bf16[224,256]{1,0:T(8,128)(2,1)S(1)} %shard_map.81), channel_id=2, replica_groups=mesh['z'=16,'x'=4,'yl'=2,'yh'=2,'c'=2] {'yh','c'}, dimensions={0}, use_global_device_ids=true | all-gather | bytes 573440 | tf_op jit(solution)/shard_map/all_gather | solution.py:222
  117.5 0.8 shard_map.82
  (1 shorter events, 0.0 us)
Async XLA Ops:
  18.1 30.8 %copy-start = (bf16[256,256]{1,0:T(8,128)(2,1)S(1)}, bf16[256,256]{1,0:T(8,128)(2,1)}, u32[]{:S(2)}) copy-start(bf16[256,256]{1,0:T(8,128)(2,1)} %weight.1) | copy-start | bytes 393220
  91.1 15.5 %all-to-all-start.4 = ((bf16[8,136,256]{2,1,0:T(8,128)(2,1)}), bf16[8,136,256]{2,1,0:T(8,128)(2,1)S(1)}, u32[]{:S(2)}, u32[]{:S(2)}) async-start(bf16[8,136,256]{2,1,0:T(8,128)(2,1)} %shard_map.80), calls=%async_computation.4 | async-start | bytes 1114112 | tf_op jit(solution)/shard_map/all_to_all | solution.py:220
  94.6 12.0 %collective-permute-start = (bf16[32,256]{1,0:T(8,128)(2,1)S(1)}, bf16[32,256]{1,0:T(8,128)(2,1)S(1)}, u32[]{:S(2)}, u32[]{:S(2)}) collective-permute-start(bf16[32,256]{1,0:T(8,128)(2,1)S(1)} %get-tuple-element.16), channel_id=1, source_target_pairs={{0,0},{1,4},{2,8},{3,12},{4,1},{5,5},{6,9},{7,13},{8,2},{9,6},{10,... | collective-permute-start | bytes 49160 | tf_op jit(solution)/shard_map/ppermute | solution.py:213

commit v7 on v6

--- a/solution.py
+++ b/solution.py
@@ -41,11 +41,10 @@
     )(*args)
 
 
-def words_body(place_far, bits_far, features_far, grads_far, out, place, bits, features, grads, words, sems):
+def words_body(place_far, bits_far, features_far, out, place, bits, features, words, sems):
     fetches = [
         pltpu.make_async_copy(place_far, place, sems.at[0]),
         pltpu.make_async_copy(features_far, features, sems.at[1]),
-        pltpu.make_async_copy(grads_far, grads, sems.at[2]),
         pltpu.make_async_copy(bits_far, bits, sems.at[3]),
     ]
     for fetch in fetches:
@@ -62,15 +61,12 @@
         [jnp.where(want == key[0:1, c * 128 : (c + 1) * 128], 1.0, 0.0) for c in range(4)], axis=1
     ).astype(BF)
     fetches[1].wait()
-    fetches[2].wait()
     puts = []
     for k in range(K8):
-        quarter = grads.at[pl.ds((k % 4) * 32, 32), :]
         puts.append(pltpu.make_async_copy(features, out.at[k, pl.ds(32, 128), :], sems.at[4 + k]))
-        puts.append(pltpu.make_async_copy(quarter, out.at[k, pl.ds(160, 32), :], sems.at[12 + k]))
     for put in puts:
         put.start()
-    fetches[3].wait()
+    fetches[2].wait()
     dense = jnp.dot(hot, bits[...].astype(F32).astype(BF), preferred_element_type=F32).astype(BF)
     for k in range(K8):
         words[k, :, 0:128] = dense[k * 64 : k * 64 + 32]
@@ -108,12 +104,11 @@
         lanes = degree[0:8, (z // 4) * 128 : (z // 4 + 1) * 128]
         out[z] = jnp.concatenate([mine[:, 0:128], mine[:, 128:256], lanes], axis=0).astype(BF)
     x1, q, r = where_am_i()
-    own[0:32, :] = plane[x1 * 4 + r, pl.ds(pl.multiple_of(32 + q * 32, 32), 32), :]
-    own[32:64, :] = plane[x1 * 4 + r, 160:192, :]
+    own[...] = plane[x1 * 4 + r, pl.ds(pl.multiple_of(32 + q * 32, 32), 32), :]
     turned[...] = block.T
 
 
-def middle_body(parts, own, weight, act, back, pushed, term):
+def middle_body(parts, own, grads, weight, act, back, pushed, term):
     total = jnp.sum(parts[...].astype(F32), axis=0)
     degree = jnp.sum(total[64:68], axis=0, keepdims=True)
     first = (lax.axis_index("z") % 4) * 32
@@ -121,11 +116,11 @@
     counted = jnp.sum(jnp.where(pick, degree, 0.0), axis=1, keepdims=True)
     scaling = lax.rsqrt(1.0 + counted)
     gathered = jnp.concatenate([total[0:32], total[32:64]], axis=1)
-    hidden = (own[0:32, :].astype(F32) + gathered * scaling).astype(BF)
+    hidden = (own[...].astype(F32) + gathered * scaling).astype(BF)
     logits = jnp.dot(hidden, weight[...], preferred_element_type=F32)
     gate = jax.nn.sigmoid(logits)
     act[...] = (logits * gate).astype(BF)
-    upstream = (own[32:64, :].astype(F32) * gate * (1.0 + logits * (1.0 - gate))).astype(BF)
+    upstream = (grads[...].astype(F32) * gate * (1.0 + logits * (1.0 - gate))).astype(BF)
     hidden_grad = lax.dot_general(
         upstream, weight[...], (((1,), (1,)), ((), ())), preferred_element_type=F32
     )
@@ -174,25 +169,26 @@
     near, far = pl.BlockSpec(memory_space=pltpu.VMEM), pl.BlockSpec(memory_space=pltpu.HBM)
     plane = pl.pallas_call(
         words_body,
-        out_shape=jax.ShapeDtypeStruct((K8, 192, W), BF),
-        in_specs=[far] * 4,
+        out_shape=jax.ShapeDtypeStruct((K8, 160, W), BF),
+        in_specs=[far] * 3,
         out_specs=far,
         scratch_shapes=[
             pltpu.VMEM((1, 32), I32),
             pltpu.VMEM((512, 128), I32),
             pltpu.VMEM((128, W), BF),
-            pltpu.VMEM((128, W), BF),
             pltpu.VMEM((K8, 32, W), BF),
             pltpu.SemaphoreType.DMA((21,)),
         ],
         compiler_params=pltpu.CompilerParams(vmem_limit_bytes=FULL),
-    )(back_place.reshape(1, 32), back_bits.reshape(512, 128), features, out_grad)
+    )(back_place.reshape(1, 32), back_bits.reshape(512, 128), features)
     plane = lax.all_to_all(plane, ROWS2, 0, 0)
+    _, _, r = where_am_i()
+    grads = lax.ppermute(lax.dynamic_slice_in_dim(out_grad, r * Q, Q, 0), PLANE, swap_pairs())
     parts, own, turned = call(
         forward_body,
         (
             jax.ShapeDtypeStruct((Z, 72, 128), BF),
-            jax.ShapeDtypeStruct((2 * Q, W), BF),
+            jax.ShapeDtypeStruct((Q, W), BF),
             jax.ShapeDtypeStruct((K8 * 128, Z * Q), BF),
         ),
         plane,
@@ -208,6 +204,7 @@
         ),
         parts,
         own,
+        grads,
         weight,
     )
     act = lax.ppermute(act, PLANE, swap_pairs())

time: 119 us -> 119 us (level)
  blocking collectives: 96.6 us -> 65.7 us
  starting transfers between devices: 13.8 us -> 35.8 us
  waiting for transfers between devices: 1.71 us -> 9.66 us
    all_to_all x1 -> x0, blocking collectives: 30.7 us -> none  [per_device(): parts = lax.all_to_all(parts, 'z', 0, 0)]
    all_to_all x0 -> x1, starting transfers between devices: none -> 16.9 us  [per_device(): parts = lax.all_to_all(parts, 'z', 0, 0)]
    all_to_all x0 -> x1, waiting for transfers between devices: none -> 6.55 us  [per_device(): parts = lax.all_to_all(parts, 'z', 0, 0)]
    ppermute x0 -> x1, starting transfers between devices: none -> 5.08 us  [per_device(): lax.ppermute(lax.dynamic_slice_in_dim(out_grad, r * Q, Q, 0), PLANE, swap...]
    ppermute x0 -> x1, waiting for transfers between devices: none -> 1.41 us  [per_device(): lax.ppermute(lax.dynamic_slice_in_dim(out_grad, r * Q, Q, 0), PLANE, swap...]
  transfers between devices with their start and end apart: 2 -> 4, of which waited for: 1 -> 3; matrix products, arithmetic and copies ran while one was open for 0% -> 0% of each run, Pallas kernels for 0% -> 0%
where the time goes in v7:
time: 119 us; the launch traced here: 118 us
  blocking collectives  65.7 us (55%)
  starting transfers between devices  35.8 us (30%)
  waiting for transfers between devices  9.66 us (8%)
  Pallas kernels  6.19 us (5%)
    all_to_all x1, blocking collectives, per_device(): gathered = lax.all_to_all(sent, 'z', 0, 0)  20.5 us
    all_to_all x1, blocking collectives, per_device(): terms = lax.all_to_all(term.reshape(PL, 8, W), PLANE, 0, 0)  20.4 us
    all_to_all x1, starting transfers between devices, per_device(): parts = lax.all_to_all(parts, 'z', 0, 0)  16.9 us
    all_to_all x1, blocking collectives, per_device(): plane = lax.all_to_all(plane, ROWS2, 0, 0)  14 us
    all_gather x1, blocking collectives, per_device(): shares = lax.all_gather(share, REP, axis=0)  10.8 us
    ppermute x1, starting transfers between devices, per_device(): act = lax.ppermute(act, PLANE, swap_pairs())  10.2 us
    all_to_all x1, waiting for transfers between devices, per_device(): parts = lax.all_to_all(parts, 'z', 0, 0)  6.55 us
    ppermute x1, starting transfers between devices, per_device(): lax.ppermute(lax.dynamic_slice_in_dim(out_grad, r * Q, Q, 0), PLANE, swap...  5.08 us
  transfers between devices with their start and end apart: 4, of which 3 were waited for; matrix products, arithmetic and copies ran while one was open for 0% of the time, Pallas kernels for 0%

profile of v7, /device:TPU:1, one launch (start us, length us, event | category | flops | bytes accessed | tf_op | source)
XLA Modules:
  0.0 118.1 jit_solution(934779503995101224)
XLA Ops:
  0.6 0.0 copy-start
  0.6 2.2 %shard_map.76 = bf16[8,160,256]{2,1,0:T(8,128)(2,1)} custom-call(s32[1,32]{1,0:T(1,128)} %bitcast.7, s32[512,128]{1,0:T(8,128)} %bitcast.6, bf16[128,256]{1,0:T(8,128)(2,1)} %features_far.1), custom_call_target="tpu_custom_call" | custom-call | tf_op jit(solution)/shard_map/pallas_call | solution.py:170
  2.8 14.0 %all_to_all.25.plane = bf16[8,160,256]{2,1,0:T(8,128)(2,1)S(1)} all-to-all(bf16[8,160,256]{2,1,0:T(8,128)(2,1)} %shard_map.76), channel_id=1, replica_groups=mesh['z'=16,'x'=4,'yl'=2,'yh'=2,'c'=2] {'x','yl'}, dimensions={0} | all-to-all | bytes 1310720 | tf_op jit(solution)/shard_map/all_to_all | solution.py:184
  16.9 1.5 %shard_map.77 = (bf16[16,72,128]{2,1,0:T(8,128)(2,1)}, bf16[32,256]{1,0:T(8,128)(2,1)S(1)}, bf16[1024,512]{1,0:T(8,128)(2,1)S(1)}) custom-call(bf16[8,160,256]{2,1,0:T(8,128)(2,1)S(1)} %all_to_all.25.plane), custom_call_target="tpu_custom_call" | custom-call | tf_op jit(solution)/shard_map/pallas_call | solution.py:35
  18.3 0.0 copy-start.1
  18.3 16.9 %all-to-all-start.1 = ((bf16[16,72,128]{2,1,0:T(8,128)(2,1)}), bf16[16,72,128]{2,1,0:T(8,128)(2,1)S(1)}, u32[]{:S(2)}, u32[]{:S(2)}) async-start(bf16[16,72,128]{2,1,0:T(8,128)(2,1)} %get-tuple-element.11), calls=%async_computation.1 | async-start | bytes 589824 | tf_op jit(solution)/shard_map/all_to_all | solution.py:196
  35.2 0.0 copy-done
  35.3 5.1 %collective-permute-start = (bf16[32,256]{1,0:T(8,128)(2,1)S(1)}, bf16[32,256]{1,0:T(8,128)(2,1)S(1)}, u32[]{:S(2)}, u32[]{:S(2)}) collective-permute-start(bf16[32,256]{1,0:T(8,128)(2,1)S(1)} %constant_dynamic-slice_fusion), channel_id=1, source_target_pairs={{0,0},{1,4},{2,8},{3,12},{4,1},{5,5},{6,9},{7,13},{8,2},{9,6},{10,... | collective-permute-start | bytes 49160 | tf_op jit(solution)/shard_map/ppermute | solution.py:186
  40.4 1.4 %collective-permute-done.grads = bf16[32,256]{1,0:T(8,128)(2,1)S(1)} collective-permute-done((bf16[32,256]{1,0:T(8,128)(2,1)S(1)}, bf16[32,256]{1,0:T(8,128)(2,1)S(1)}, u32[]{:S(2)}, u32[]{:S(2)}) %collective-permute-start) | collective-permute-done | bytes 16416 | tf_op jit(solution)/shard_map/ppermute | solution.py:186
  41.8 6.5 %all-to-all-done.1.parts = bf16[16,72,128]{2,1,0:T(8,128)(2,1)S(1)} async-done(((bf16[16,72,128]{2,1,0:T(8,128)(2,1)}), bf16[16,72,128]{2,1,0:T(8,128)(2,1)S(1)}, u32[]{:S(2)}, u32[]{:S(2)}) %all-to-all-start.1) | async-done | bytes 294944 | tf_op jit(solution)/shard_map/all_to_all | solution.py:196
  48.3 0.0 copy-done.1
  48.3 0.4 shard_map.78
  48.7 20.4 %all_to_all.26.terms = bf16[32,8,256]{2,1,0:T(8,128)(2,1)S(1)} all-to-all(bf16[32,8,256]{2,1,0:T(8,128)(2,1)S(1)} %bitcast.5), channel_id=1, replica_groups=mesh['z'=16,'x'=4,'yl'=2,'yh'=2,'c'=2] {'x','yl','yh','c'}, dimensions={0} | all-to-all | bytes 262144 | tf_op jit(solution)/shard_map/all_to_all | solution.py:211
  69.2 20.5 %all_to_all.27.gathered = bf16[16,40,256]{2,1,0:T(8,128)(2,1)S(1)} all-to-all(bf16[16,40,256]{2,1,0:T(8,128)(2,1)S(1)} %shard_map.79), channel_id=1, replica_groups=mesh['z'=16,'x'=4,'yl'=2,'yh'=2,'c'=2] {'z'}, dimensions={0} | all-to-all | bytes 655360 | tf_op jit(solution)/shard_map/all_to_all | solution.py:213
  89.6 1.3 %shard_map.80 = bf16[8,136,256]{2,1,0:T(8,128)(2,1)} custom-call(bf16[1024,512]{1,0:T(8,128)(2,1)S(1)} %get-tuple-element.10.turned, bf16[16,40,256]{2,1,0:T(8,128)(2,1)S(1)} %all_to_all.27.gathered, f32[32,256]{1,0:T(8,128)S(1)} %get-tuple-element.15.hidden_grad), custom_call_target="tpu_custom_call" | custom-call | tf_op jit(solution)/shard_map/pallas_call | solution.py:35
  90.9 3.5 %all-to-all-start.4 = ((bf16[8,136,256]{2,1,0:T(8,128)(2,1)}), bf16[8,136,256]{2,1,0:T(8,128)(2,1)S(1)}, u32[]{:S(2)}, u32[]{:S(2)}) async-start(bf16[8,136,256]{2,1,0:T(8,128)(2,1)} %shard_map.80), calls=%async_computation.4 | async-start | bytes 1114112 | tf_op jit(solution)/shard_map/all_to_all | solution.py:217
  94.4 10.2 %collective-permute-start.1 = (bf16[32,256]{1,0:T(8,128)(2,1)S(1)}, bf16[32,256]{1,0:T(8,128)(2,1)S(1)}, u32[]{:S(2)}, u32[]{:S(2)}) collective-permute-start(bf16[32,256]{1,0:T(8,128)(2,1)S(1)} %get-tuple-element.16), channel_id=1, source_target_pairs={{0,0},{1,4},{2,8},{3,12},{4,1},{5,5},{6,9},{7,13},{8,2},{9,6},{10,... | collective-permute-start | bytes 49160 | tf_op jit(solution)/shard_map/ppermute | solution.py:210
  104.7 1.7 %collective-permute-done.1.act = bf16[32,256]{1,0:T(8,128)(2,1)S(1)} collective-permute-done((bf16[32,256]{1,0:T(8,128)(2,1)S(1)}, bf16[32,256]{1,0:T(8,128)(2,1)S(1)}, u32[]{:S(2)}, u32[]{:S(2)}) %collective-permute-start.1) | collective-permute-done | bytes 16416 | tf_op jit(solution)/shard_map/ppermute | solution.py:210
  106.4 0.0 all-to-all-done.4.parts
  106.4 0.1 shard_map.81
  106.5 10.8 %all-gather = bf16[896,256]{1,0:T(8,128)(2,1)S(1)} all-gather(bf16[224,256]{1,0:T(8,128)(2,1)S(1)} %shard_map.81), channel_id=2, replica_groups=mesh['z'=16,'x'=4,'yl'=2,'yh'=2,'c'=2] {'yh','c'}, dimensions={0}, use_global_device_ids=true | all-gather | bytes 573440 | tf_op jit(solution)/shard_map/all_gather | solution.py:219
  117.3 0.8 shard_map.82
  (2 shorter events, 0.1 us)
Async XLA Ops:
  0.6 34.6 %copy-start = (bf16[128,256]{1,0:T(8,128)(2,1)S(1)}, bf16[128,256]{1,0:T(8,128)(2,1)}, u32[]{:S(2)}) copy-start(bf16[128,256]{1,0:T(8,128)(2,1)} %param.9) | copy-start | bytes 196612
  18.3 30.0 %copy-start.1 = (bf16[256,256]{1,0:T(8,128)(2,1)S(1)}, bf16[256,256]{1,0:T(8,128)(2,1)}, u32[]{:S(2)}) copy-start(bf16[256,256]{1,0:T(8,128)(2,1)} %weight.1) | copy-start | bytes 393220
  18.3 30.0 %all-to-all-start.1 = ((bf16[16,72,128]{2,1,0:T(8,128)(2,1)}), bf16[16,72,128]{2,1,0:T(8,128)(2,1)S(1)}, u32[]{:S(2)}, u32[]{:S(2)}) async-start(bf16[16,72,128]{2,1,0:T(8,128)(2,1)} %get-tuple-element.11), calls=%async_computation.1 | async-start | bytes 589824 | tf_op jit(solution)/shard_map/all_to_all | solution.py:196
  35.3 6.5 %collective-permute-start = (bf16[32,256]{1,0:T(8,128)(2,1)S(1)}, bf16[32,256]{1,0:T(8,128)(2,1)S(1)}, u32[]{:S(2)}, u32[]{:S(2)}) collective-permute-start(bf16[32,256]{1,0:T(8,128)(2,1)S(1)} %constant_dynamic-slice_fusion), channel_id=1, source_target_pairs={{0,0},{1,4},{2,8},{3,12},{4,1},{5,5},{6,9},{7,13},{8,2},{9,6},{10,... | collective-permute-start | bytes 49160 | tf_op jit(solution)/shard_map/ppermute | solution.py:186
  90.9 15.5 %all-to-all-start.4 = ((bf16[8,136,256]{2,1,0:T(8,128)(2,1)}), bf16[8,136,256]{2,1,0:T(8,128)(2,1)S(1)}, u32[]{:S(2)}, u32[]{:S(2)}) async-start(bf16[8,136,256]{2,1,0:T(8,128)(2,1)} %shard_map.80), calls=%async_computation.4 | async-start | bytes 1114112 | tf_op jit(solution)/shard_map/all_to_all | solution.py:217
  94.4 11.9 %collective-permute-start.1 = (bf16[32,256]{1,0:T(8,128)(2,1)S(1)}, bf16[32,256]{1,0:T(8,128)(2,1)S(1)}, u32[]{:S(2)}, u32[]{:S(2)}) collective-permute-start(bf16[32,256]{1,0:T(8,128)(2,1)S(1)} %get-tuple-element.16), channel_id=1, source_target_pairs={{0,0},{1,4},{2,8},{3,12},{4,1},{5,5},{6,9},{7,13},{8,2},{9,6},{10,... | collective-permute-start | bytes 49160 | tf_op jit(solution)/shard_map/ppermute | solution.py:210

commit v8 on v7

--- a/solution.py
+++ b/solution.py
@@ -136,7 +136,8 @@
         out[z] = message
 
 
-def backward_body(turned, gathered, hidden_grad, out):
+def backward_body(turned, gathered, hidden_grad, act, out, kept):
+    kept[...] = act[...]
     x1, q, r = where_am_i()
     received = gathered[...]
     source = received[:, 0:32].reshape(Z * Q, W)
@@ -211,8 +212,13 @@
     terms = lax.all_to_all(term.reshape(PL, 8, W), PLANE, 0, 0)
     sent = call(send_body, jax.ShapeDtypeStruct((Z, 40, W), BF), terms, pushed)
     gathered = lax.all_to_all(sent, "z", 0, 0)
-    parts = call(
-        backward_body, jax.ShapeDtypeStruct((K8, 136, W), BF), turned, gathered, hidden_grad
+    parts, act = call(
+        backward_body,
+        (jax.ShapeDtypeStruct((K8, 136, W), BF), jax.ShapeDtypeStruct((Q, W), BF)),
+        turned,
+        gathered,
+        hidden_grad,
+        act,
     )
     parts = lax.all_to_all(parts, ROWS2, 0, 0)
     share = call(share_body, jax.ShapeDtypeStruct((224, W), BF), parts, act)

time: 119 us -> 118 us (level)
  waiting for transfers between devices: 9.66 us -> 20.4 us
  starting transfers between devices: 35.8 us -> 30.2 us
  blocking collectives: 65.7 us -> 60.4 us
    all_to_all x1, blocking collectives: 20.5 us -> 10.3 us  [per_device(): parts = lax.all_to_all(parts, ROWS2, 0, 0)]
    all_to_all x1, waiting for transfers between devices: 0.01 us -> 10.1 us  [per_device(): gathered = lax.all_to_all(sent, 'z', 0, 0)]
    ppermute x1, starting transfers between devices: 10.2 us -> 2.66 us  [per_device(): act = lax.ppermute(act, PLANE, swap_pairs())]
    all_gather x1, blocking collectives: 10.8 us -> 15.7 us  [per_device(): shares = lax.all_gather(share, REP, axis=0)]
    all_to_all x1, starting transfers between devices: 3.54 us -> 5.53 us  [per_device(): gathered = lax.all_to_all(sent, 'z', 0, 0)]
  transfers between devices with their start and end apart: 4 -> 4, of which waited for: 3 -> 4; matrix products, arithmetic and copies ran while one was open for 0% -> 0% of each run, Pallas kernels for 0% -> 0%
where the time goes in v8:
time: 118 us
  blocking collectives  60.4 us (51%)
  starting transfers between devices  30.2 us (26%)
  waiting for transfers between devices  20.4 us (17%)
  Pallas kernels  6.11 us (5%)
    all_to_all x1, blocking collectives, per_device(): terms = lax.all_to_all(term.reshape(PL, 8, W), PLANE, 0, 0)  20.4 us
    all_to_all x1, starting transfers between devices, per_device(): parts = lax.all_to_all(parts, 'z', 0, 0)  16.9 us
    all_gather x1, blocking collectives, per_device(): shares = lax.all_gather(share, REP, axis=0)  15.7 us
    all_to_all x1, blocking collectives, per_device(): plane = lax.all_to_all(plane, ROWS2, 0, 0)  14 us
    all_to_all x1, blocking collectives, per_device(): parts = lax.all_to_all(parts, ROWS2, 0, 0)  10.3 us
    all_to_all x1, waiting for transfers between devices, per_device(): gathered = lax.all_to_all(sent, 'z', 0, 0)  10.1 us
    all_to_all x1, waiting for transfers between devices, per_device(): parts = lax.all_to_all(parts, 'z', 0, 0)  6.55 us
    all_to_all x1, starting transfers between devices, per_device(): gathered = lax.all_to_all(sent, 'z', 0, 0)  5.53 us
  transfers between devices with their start and end apart: 4, of which 4 were waited for; matrix products, arithmetic and copies ran while one was open for 0% of the time, Pallas kernels for 0%

profile of v8, /device:TPU:1, one launch (start us, length us, event | category | flops | bytes accessed | tf_op | source)
XLA Modules:
  0.0 117.9 jit_solution(11518193077749957465)
XLA Ops:
  0.6 0.0 copy-start
  0.6 2.2 %shard_map.76 = bf16[8,160,256]{2,1,0:T(8,128)(2,1)} custom-call(s32[1,32]{1,0:T(1,128)} %bitcast.7, s32[512,128]{1,0:T(8,128)} %bitcast.6, bf16[128,256]{1,0:T(8,128)(2,1)} %features_far.1), custom_call_target="tpu_custom_call" | custom-call | tf_op jit(solution)/shard_map/pallas_call | solution.py:171
  2.8 14.0 %all_to_all.25.plane = bf16[8,160,256]{2,1,0:T(8,128)(2,1)S(1)} all-to-all(bf16[8,160,256]{2,1,0:T(8,128)(2,1)} %shard_map.76), channel_id=1, replica_groups=mesh['z'=16,'x'=4,'yl'=2,'yh'=2,'c'=2] {'x','yl'}, dimensions={0} | all-to-all | bytes 1310720 | tf_op jit(solution)/shard_map/all_to_all | solution.py:185
  16.9 1.5 %shard_map.77 = (bf16[16,72,128]{2,1,0:T(8,128)(2,1)}, bf16[32,256]{1,0:T(8,128)(2,1)S(1)}, bf16[1024,512]{1,0:T(8,128)(2,1)S(1)}) custom-call(bf16[8,160,256]{2,1,0:T(8,128)(2,1)S(1)} %all_to_all.25.plane), custom_call_target="tpu_custom_call" | custom-call | tf_op jit(solution)/shard_map/pallas_call | solution.py:35
  18.3 0.0 copy-start.1
  18.3 16.9 %all-to-all-start.1 = ((bf16[16,72,128]{2,1,0:T(8,128)(2,1)}), bf16[16,72,128]{2,1,0:T(8,128)(2,1)S(1)}, u32[]{:S(2)}, u32[]{:S(2)}) async-start(bf16[16,72,128]{2,1,0:T(8,128)(2,1)} %get-tuple-element.13), calls=%async_computation.1 | async-start | bytes 589824 | tf_op jit(solution)/shard_map/all_to_all | solution.py:197
  35.2 0.0 copy-done
  35.3 5.1 %collective-permute-start = (bf16[32,256]{1,0:T(8,128)(2,1)S(1)}, bf16[32,256]{1,0:T(8,128)(2,1)S(1)}, u32[]{:S(2)}, u32[]{:S(2)}) collective-permute-start(bf16[32,256]{1,0:T(8,128)(2,1)S(1)} %constant_dynamic-slice_fusion), channel_id=1, source_target_pairs={{0,0},{1,4},{2,8},{3,12},{4,1},{5,5},{6,9},{7,13},{8,2},{9,6},{10,... | collective-permute-start | bytes 49160 | tf_op jit(solution)/shard_map/ppermute | solution.py:187
  40.3 1.4 %collective-permute-done.grads = bf16[32,256]{1,0:T(8,128)(2,1)S(1)} collective-permute-done((bf16[32,256]{1,0:T(8,128)(2,1)S(1)}, bf16[32,256]{1,0:T(8,128)(2,1)S(1)}, u32[]{:S(2)}, u32[]{:S(2)}) %collective-permute-start) | collective-permute-done | bytes 16416 | tf_op jit(solution)/shard_map/ppermute | solution.py:187
  41.8 6.6 %all-to-all-done.1.parts = bf16[16,72,128]{2,1,0:T(8,128)(2,1)S(1)} async-done(((bf16[16,72,128]{2,1,0:T(8,128)(2,1)}), bf16[16,72,128]{2,1,0:T(8,128)(2,1)S(1)}, u32[]{:S(2)}, u32[]{:S(2)}) %all-to-all-start.1) | async-done | bytes 294944 | tf_op jit(solution)/shard_map/all_to_all | solution.py:197
  48.3 0.0 copy-done.1
  48.3 0.4 shard_map.78
  48.7 20.4 %all_to_all.26.terms = bf16[32,8,256]{2,1,0:T(8,128)(2,1)S(1)} all-to-all(bf16[32,8,256]{2,1,0:T(8,128)(2,1)S(1)} %bitcast.5), channel_id=1, replica_groups=mesh['z'=16,'x'=4,'yl'=2,'yh'=2,'c'=2] {'x','yl','yh','c'}, dimensions={0} | all-to-all | bytes 262144 | tf_op jit(solution)/shard_map/all_to_all | solution.py:212
  69.1 0.8 shard_map.79
  69.9 5.5 %all-to-all-start.3 = ((bf16[16,40,256]{2,1,0:T(8,128)(2,1)}), bf16[16,40,256]{2,1,0:T(8,128)(2,1)S(1)}, u32[]{:S(2)}, u32[]{:S(2)}) async-start(bf16[16,40,256]{2,1,0:T(8,128)(2,1)} %shard_map.79), calls=%async_computation.3 | async-start | bytes 655360 | tf_op jit(solution)/shard_map/all_to_all | solution.py:214
  75.5 2.7 %collective-permute-start.1 = (bf16[32,256]{1,0:T(8,128)(2,1)S(1)}, bf16[32,256]{1,0:T(8,128)(2,1)S(1)}, u32[]{:S(2)}, u32[]{:S(2)}) collective-permute-start(bf16[32,256]{1,0:T(8,128)(2,1)S(1)} %get-tuple-element.18), channel_id=1, source_target_pairs={{0,0},{1,4},{2,8},{3,12},{4,1},{5,5},{6,9},{7,13},{8,2},{9,6},{10,... | collective-permute-start | bytes 49160 | tf_op jit(solution)/shard_map/ppermute | solution.py:211
  78.1 2.4 %collective-permute-done.1.act = bf16[32,256]{1,0:T(8,128)(2,1)S(1)} collective-permute-done((bf16[32,256]{1,0:T(8,128)(2,1)S(1)}, bf16[32,256]{1,0:T(8,128)(2,1)S(1)}, u32[]{:S(2)}, u32[]{:S(2)}) %collective-permute-start.1) | collective-permute-done | bytes 16416 | tf_op jit(solution)/shard_map/ppermute | solution.py:211
  80.5 10.1 %all-to-all-done.3.gathered = bf16[16,40,256]{2,1,0:T(8,128)(2,1)S(1)} async-done(((bf16[16,40,256]{2,1,0:T(8,128)(2,1)}), bf16[16,40,256]{2,1,0:T(8,128)(2,1)S(1)}, u32[]{:S(2)}, u32[]{:S(2)}) %all-to-all-start.3) | async-done | bytes 327712 | tf_op jit(solution)/shard_map/all_to_all | solution.py:214
  90.6 0.4 shard_map.80
  91.0 10.3 %all_to_all.27.parts = bf16[8,136,256]{2,1,0:T(8,128)(2,1)S(1)} all-to-all(bf16[8,136,256]{2,1,0:T(8,128)(2,1)S(1)} %get-tuple-element.19), channel_id=1, replica_groups=mesh['z'=16,'x'=4,'yl'=2,'yh'=2,'c'=2] {'x','yl'}, dimensions={0} | all-to-all | bytes 1114112 | tf_op jit(solution)/shard_map/all_to_all | solution.py:223
  101.3 0.1 shard_map.81
  101.4 15.7 %all-gather = bf16[896,256]{1,0:T(8,128)(2,1)S(1)} all-gather(bf16[224,256]{1,0:T(8,128)(2,1)S(1)} %shard_map.81), channel_id=2, replica_groups=mesh['z'=16,'x'=4,'yl'=2,'yh'=2,'c'=2] {'yh','c'}, dimensions={0}, use_global_device_ids=true | all-gather | bytes 573440 | tf_op jit(solution)/shard_map/all_gather | solution.py:225
  117.1 0.8 shard_map.82
  (1 shorter events, 0.0 us)
Async XLA Ops:
  0.6 34.6 %copy-start = (bf16[128,256]{1,0:T(8,128)(2,1)S(1)}, bf16[128,256]{1,0:T(8,128)(2,1)}, u32[]{:S(2)}) copy-start(bf16[128,256]{1,0:T(8,128)(2,1)} %param.9) | copy-start | bytes 196612
  18.3 30.0 %copy-start.1 = (bf16[256,256]{1,0:T(8,128)(2,1)S(1)}, bf16[256,256]{1,0:T(8,128)(2,1)}, u32[]{:S(2)}) copy-start(bf16[256,256]{1,0:T(8,128)(2,1)} %weight.1) | copy-start | bytes 393220
  18.3 30.0 %all-to-all-start.1 = ((bf16[16,72,128]{2,1,0:T(8,128)(2,1)}), bf16[16,72,128]{2,1,0:T(8,128)(2,1)S(1)}, u32[]{:S(2)}, u32[]{:S(2)}) async-start(bf16[16,72,128]{2,1,0:T(8,128)(2,1)} %get-tuple-element.13), calls=%async_computation.1 | async-start | bytes 589824 | tf_op jit(solution)/shard_map/all_to_all | solution.py:197
  35.3 6.5 %collective-permute-start = (bf16[32,256]{1,0:T(8,128)(2,1)S(1)}, bf16[32,256]{1,0:T(8,128)(2,1)S(1)}, u32[]{:S(2)}, u32[]{:S(2)}) collective-permute-start(bf16[32,256]{1,0:T(8,128)(2,1)S(1)} %constant_dynamic-slice_fusion), channel_id=1, source_target_pairs={{0,0},{1,4},{2,8},{3,12},{4,1},{5,5},{6,9},{7,13},{8,2},{9,6},{10,... | collective-permute-start | bytes 49160 | tf_op jit(solution)/shard_map/ppermute | solution.py:187
  69.9 20.7 %all-to-all-start.3 = ((bf16[16,40,256]{2,1,0:T(8,128)(2,1)}), bf16[16,40,256]{2,1,0:T(8,128)(2,1)S(1)}, u32[]{:S(2)}, u32[]{:S(2)}) async-start(bf16[16,40,256]{2,1,0:T(8,128)(2,1)} %shard_map.79), calls=%async_computation.3 | async-start | bytes 655360 | tf_op jit(solution)/shard_map/all_to_all | solution.py:214
  75.5 5.1 %collective-permute-start.1 = (bf16[32,256]{1,0:T(8,128)(2,1)S(1)}, bf16[32,256]{1,0:T(8,128)(2,1)S(1)}, u32[]{:S(2)}, u32[]{:S(2)}) collective-permute-start(bf16[32,256]{1,0:T(8,128)(2,1)S(1)} %get-tuple-element.18), channel_id=1, source_target_pairs={{0,0},{1,4},{2,8},{3,12},{4,1},{5,5},{6,9},{7,13},{8,2},{9,6},{10,... | collective-permute-start | bytes 49160 | tf_op jit(solution)/shard_map/ppermute | solution.py:211
